TPU v7x, 256 devices: a whole 4x4x8 slice. The times are simulated.
256 devices in a mesh: blk: 32 (over z, x_hi, core), rep: 2 (over x_lo), feat: 4 (over y).
Axes of the slice: x: 4 (x_hi: 2, x_lo: 2; x = x_hi * 2 + x_lo), y: 4, z: 8, core: 2. Of those that a mesh axis runs over, the one named last changes fastest.
Arguments:
- features_t: bfloat16 [256, 16384], P('feat', 'blk'), may hold values from -6 to 6
- tile_values: bfloat16 [32, 32, 12, 128, 128], P('blk'), may hold values from 0 to 0.015319824
- tile_rows: int32 [32, 32, 12], P('blk'), may hold values from 0 to 3
- tile_cols: int32 [32, 32, 12], P('blk'), may hold values from 0 to 3
- tile_count: int32 [32, 32], P('blk'), may hold values from 1 to 12, as said below
- weight: bfloat16 [256, 256], P('feat'), may hold values from -0.375 to 0.375
- cotangent_t: bfloat16 [256, 16384], P('feat', 'blk'), may hold values from -6 to 6
Outputs:
- hidden_t: bfloat16 [256, 16384], P('feat', 'blk')
- weight_grad: float32 [256, 256], P('feat')
- input_grad_t: bfloat16 [256, 16384], P('feat', 'blk')
Inputs may be any that keep to these rules, and one draw needn't show every extreme that they name: `tile_count`: section 0 (a partition's own tiles) always has 12 live slots; section k > 0 has between (c + 1) // 2 and c live slots, with c = max(1, 12 * (64 - k) // 64). `tile_rows`: several live tiles of a section may share a destination block or a source block.
All inputs are finite; a program needn't handle non-finite values.
Results may differ from a plain program's by a relative error of at most 0.027.
Values may be sent and summed in bfloat16 or wider, within the bound.
A program may use at most 128 MiB of HBM per device.

v0:
```python
import jax
import jax.numpy as jnp
from jax import lax
from jax.sharding import PartitionSpec as P

slot_group = 4


def passed_along(block, axis, distance):
    devices = range(lax.axis_size(axis))
    route = [((i - distance) % len(devices), i) for i in devices]
    return lax.ppermute(block, axis, route)


def tile_pass(buffer, running, tile_set, pick_ids, put_ids, filled, transpose):
    feature_rows = buffer.shape[0]
    tile_edge = tile_set.shape[-1]
    block_count = buffer.shape[1] // tile_edge
    source = buffer.reshape(feature_rows, block_count, tile_edge)
    level_ids = jnp.arange(block_count, dtype=jnp.int32)

    def one_turn(turn_index, carried):
        first_slot = turn_index * slot_group
        tile_group = lax.dynamic_slice_in_dim(tile_set, first_slot, slot_group, 0)
        pick_group = lax.dynamic_slice_in_dim(pick_ids, first_slot, slot_group, 0)
        put_group = lax.dynamic_slice_in_dim(put_ids, first_slot, slot_group, 0)
        live_mask = (first_slot + jnp.arange(slot_group, dtype=jnp.int32) < filled).astype(
            jnp.float32
        )
        chosen = jnp.take(source, pick_group, axis=1)
        if transpose:
            products = jnp.einsum(
                "fgi,gij->gfj", chosen, tile_group, preferred_element_type=jnp.float32
            )
        else:
            products = jnp.einsum(
                "fgj,gij->gfi", chosen, tile_group, preferred_element_type=jnp.float32
            )
        spread = (put_group[:, None] == level_ids[None, :]).astype(jnp.float32) * live_mask[:, None]
        return carried + jnp.einsum("gb,gfi->fbi", spread, products).reshape(carried.shape)

    turn_count = (filled + slot_group - 1) // slot_group
    return lax.fori_loop(0, turn_count, one_turn, running)


def section_arrays(tile_set, row_ids, col_ids, counts, section):
    return (
        lax.dynamic_index_in_dim(tile_set, section, 0, False),
        lax.dynamic_index_in_dim(row_ids, section, 0, False),
        lax.dynamic_index_in_dim(col_ids, section, 0, False),
        lax.dynamic_index_in_dim(counts, section, 0, False),
    )


def body(features_t, tile_values, tile_rows, tile_cols, tile_count, weight, cotangent_t):
    partitions = lax.axis_size("blk")
    replica = lax.axis_index("rep")
    feature_rows = features_t.shape[0]
    node_rows = features_t.shape[1]
    tile_set = tile_values[0]
    row_ids = tile_rows[0]
    col_ids = tile_cols[0]
    counts = tile_count[0]
    section_count = partitions // 2
    stride = 1
    first_section = replica * section_count
    is_second = replica == 1
    zero_field = jnp.zeros((feature_rows, node_rows), jnp.float32)

    def forward_section(buffer, running, section):
        tiles_now, rows_now, cols_now, filled = section_arrays(
            tile_set, row_ids, col_ids, counts, section
        )
        return tile_pass(buffer, running, tiles_now, cols_now, rows_now, filled, False)

    jumped = passed_along(features_t, "blk", section_count)
    current = jnp.where(is_second, jumped, features_t)
    running = forward_section(current, zero_field, first_section)

    def forward_turn(section_step, carried):
        buffer, partial_sum = carried
        buffer = passed_along(buffer, "blk", stride)
        return (buffer, forward_section(buffer, partial_sum, first_section + section_step * stride))

    current, running = lax.fori_loop(1, section_count, forward_turn, (current, running))
    aggregated = lax.psum(running, "rep").astype(jnp.bfloat16)
    columns = weight
    pre_act = lax.psum_scatter(
        lax.dot_general(
            columns, aggregated, (((0,), (0,)), ((), ())), preferred_element_type=jnp.float32
        ),
        "feat",
        scatter_dimension=0,
        tiled=True,
    )
    sigmoid_pre = jax.nn.sigmoid(pre_act)
    hidden_t = (pre_act * sigmoid_pre).astype(jnp.bfloat16)
    pre_grad = (
        cotangent_t.astype(jnp.float32) * sigmoid_pre * (1.0 + pre_act * (1.0 - sigmoid_pre))
    ).astype(jnp.bfloat16)
    gathered = lax.all_gather(pre_grad, "feat", axis=0, tiled=True)
    block_grad = lax.dot_general(
        aggregated, gathered, (((1,), (1,)), ((), ())), preferred_element_type=jnp.float32
    )
    weight_part = block_grad
    columns = weight
    signal_part = jnp.dot(columns, gathered, preferred_element_type=jnp.float32)
    weight_part, signal_part = (weight_part, signal_part)
    node_scale = float(node_rows * partitions) ** (-0.5)
    weight_grad = lax.psum((weight_part * node_scale).astype(jnp.bfloat16), "blk").astype(
        jnp.float32
    )
    signal = signal_part.astype(jnp.bfloat16)

    def backward_section(partial_sum, section):
        tiles_now, rows_now, cols_now, filled = section_arrays(
            tile_set, row_ids, col_ids, counts, section
        )
        return tile_pass(signal, partial_sum, tiles_now, rows_now, cols_now, filled, True)

    last_section = first_section + (section_count - 1) * stride
    running = backward_section(zero_field, last_section)

    def carry_turn(section_step, partial_sum):
        partial_sum = passed_along(partial_sum, "blk", -stride)
        return backward_section(partial_sum, last_section - section_step * stride)

    running = lax.fori_loop(1, section_count, carry_turn, running)
    returned = passed_along(running.astype(jnp.bfloat16), "blk", -section_count).astype(
        running.dtype
    )
    running = jnp.where(is_second, returned, running)
    input_grad_t = lax.psum(running.astype(jnp.bfloat16), "rep")
    return (hidden_t, weight_grad, input_grad_t)


def solution(mesh):
    return jax.shard_map(
        body,
        mesh=mesh,
        in_specs=(
            P("feat", "blk"),
            P("blk", None, None, None, None),
            P("blk", None, None),
            P("blk", None, None),
            P("blk", None),
            P("feat", None),
            P("feat", "blk"),
        ),
        out_specs=(P("feat", "blk"), P("feat", None), P("feat", "blk")),
        check_vma=False,
    )
```

profile of v0, /device:TPU:1, one launch (start us, length us, event | category | flops | bytes accessed | tf_op | source)
XLA Modules:
  0.0 586.3 jit_solution(9540161689045636217)
XLA Ops:
  7.2 7.8 %collective-permute-start.2 = (bf16[64,512]{1,0:T(8,128)(2,1)}, bf16[64,512]{1,0:T(8,128)(2,1)S(1)}, u32[]{:S(2)}, u32[]{:S(2)}) collective-permute-start(bf16[64,512]{1,0:T(8,128)(2,1)} %param.21), channel_id=1, source_target_pairs={{128,0},{136,8},{144,16},{152,24},{160,32},{168,40},{176,48},{184,... | collective-permute-start | bytes 196616 | tf_op jit(solution)/shard_map/ppermute | solution.py:12
  22.5 5.5 while.134
  28.0 172.0 %while.131 = (s32[]{:T(128)}, bf16[64,512]{1,0:T(8,128)(2,1)S(1)}, f32[64,512]{1,0:T(8,128)S(1)}, s32[]{:T(128)}, s32[32]{0:T(128)}, /*index=5*/bf16[32,12,128,1...) while((s32[]{:T(128)}, bf16[64,512]{1,0:T(8,128)(2,1)S(1)}, ...), condition=%wide.region_5.7_spmd, body=%wide.region_2.6_spmd.sunk | while | flops 8717408 | bytes 2299412 | solution.py:85
  34.7 5.5 while.136
  45.5 5.5 while.136
  54.5 5.5 while.136
  65.3 3.7 while.136
  77.9 5.5 while.136
  86.5 4.3 collective-permute-done.1
  90.8 3.7 while.136
  97.6 6.2 %collective-permute-done.1 = bf16[64,512]{1,0:T(8,128)(2,1)S(1)} collective-permute-done((bf16[64,512]{1,0:T(8,128)(2,1)S(1)}, bf16[64,512]{1,0:T(8,128)(2,1)S(1)}, u32[]{:S(2)}, u32[]{:S(2)}) %collective-permute-start.1) | collective-permute-done | bytes 65568 | tf_op jit(solution)/shard_map/while/body/eval_jaxpr/ppermute | solution.py:12
  103.8 3.7 while.136
  110.6 4.3 collective-permute-done.1
  114.9 5.5 while.136
  126.0 3.7 while.136
  132.8 4.3 collective-permute-done.1
  137.1 5.5 while.136
  148.2 3.7 while.136
  155.0 6.2 %collective-permute-done.1 = bf16[64,512]{1,0:T(8,128)(2,1)S(1)} collective-permute-done((bf16[64,512]{1,0:T(8,128)(2,1)S(1)}, bf16[64,512]{1,0:T(8,128)(2,1)S(1)}, u32[]{:S(2)}, u32[]{:S(2)}) %collective-permute-start.1) | collective-permute-done | bytes 65568 | tf_op jit(solution)/shard_map/while/body/eval_jaxpr/ppermute | solution.py:12
  161.2 5.5 while.136
  172.3 5.5 while.136
  180.9 4.3 collective-permute-done.1
  185.2 3.7 while.136
  192.0 4.3 collective-permute-done.1
  196.3 3.7 while.136
  200.0 6.5 %all-reduce.4 = bf16[64,512]{1,0:T(8,128)(2,1)S(1)} all-reduce(f32[64,512]{1,0:T(8,128)S(1)} %get-tuple-element.779), channel_id=1, replica_groups=mesh['blk'=32,'rep'=2,'feat'=4] {'rep'}, use_global_device_ids=true, to_apply=%region_6.8 | all-reduce | flops 32768 | bytes 196608 | tf_op jit(solution)/shard_map/psum | solution.py:86
  208.5 24.7 %reduce-scatter.4.cloned.1.call-done = f32[64,512]{1,0:T(8,128)} async-done(((f32[256,512]{1,0:T(8,128)}), f32[64,512]{1,0:T(8,128)}) %reduce-scatter.4.cloned.1.call-update) | async-done | bytes 131088 | tf_op jit(solution)/shard_map/reduce_scatter | solution.py:88
  234.8 9.7 %all_gather.3 = bf16[256,512]{1,0:T(8,128)(2,1)S(1)} all-gather(bf16[64,512]{1,0:T(8,128)(2,1)S(1)} %get-tuple-element.1108), channel_id=1, replica_groups=mesh['blk'=32,'rep'=2,'feat'=4] {'feat'}, dimensions={0}, use_global_device_ids=true | all-gather | bytes 327680 | tf_op jit(solution)/shard_map/all_gather | solution.py:101
  244.8 3.8 while.135
  248.5 186.5 %while.133 = (s32[]{:T(128)}, f32[64,512]{1,0:T(8,128)S(1)}, s32[]{:T(128)}, s32[32]{0:T(128)}, bf16[32,12,128,128]{3,2,1,0:T(8,128)(2,1)}, /*index=5*/s32[32,12...) while((s32[]{:T(128)}, f32[64,512]{1,0:T(8,128)S(1)}, ...), condition=%wide.region_14.16_spmd, body=%wide.region_11.15_spmd.sunk | while | flops 8717408 | bytes 2692628 | solution.py:128
  248.5 5.0 collective-permute-start
  268.3 5.4 while.137
  279.8 5.4 while.137
  294.9 5.2 collective-permute-start
  303.0 5.5 while.137
  318.1 5.4 collective-permute-start
  326.5 5.5 while.137
  341.9 6.9 %collective-permute-start = (f32[64,512]{1,0:T(8,128)S(1)}, f32[64,512]{1,0:T(8,128)S(1)}, u32[]{:S(2)}, u32[]{:S(2)}) collective-permute-start(f32[64,512]{1,0:T(8,128)S(1)} %get-tuple-element.1699), channel_id=1, source_target_pairs={{8,0},{16,8},{24,16},{32,24},{40,32},{48,40},{56,48},{64,56},{72,6... | collective-permute-start | bytes 393224 | tf_op jit(solution)/shard_map/while/body/eval_jaxpr/ppermute | solution.py:12
  355.5 8.7 %collective-permute-start = (f32[64,512]{1,0:T(8,128)S(1)}, f32[64,512]{1,0:T(8,128)S(1)}, u32[]{:S(2)}, u32[]{:S(2)}) collective-permute-start(f32[64,512]{1,0:T(8,128)S(1)} %get-tuple-element.1699), channel_id=1, source_target_pairs={{8,0},{16,8},{24,16},{32,24},{40,32},{48,40},{56,48},{64,56},{72,6... | collective-permute-start | bytes 393224 | tf_op jit(solution)/shard_map/while/body/eval_jaxpr/ppermute | solution.py:12
  367.2 5.5 while.137
  382.6 6.9 %collective-permute-start = (f32[64,512]{1,0:T(8,128)S(1)}, f32[64,512]{1,0:T(8,128)S(1)}, u32[]{:S(2)}, u32[]{:S(2)}) collective-permute-start(f32[64,512]{1,0:T(8,128)S(1)} %get-tuple-element.1699), channel_id=1, source_target_pairs={{8,0},{16,8},{24,16},{32,24},{40,32},{48,40},{56,48},{64,56},{72,6... | collective-permute-start | bytes 393224 | tf_op jit(solution)/shard_map/while/body/eval_jaxpr/ppermute | solution.py:12
  392.5 5.5 while.137
  404.2 5.5 while.137
  415.9 5.5 while.137
  421.4 5.1 collective-permute-start
  429.5 5.5 while.137
  435.0 4.6 collective-permute-start.3
  443.0 134.4 %psum.22 = bf16[64,256]{1,0:T(8,128)(2,1)S(1)} all-reduce(bf16[64,256]{1,0:T(8,128)(2,1)S(1)} %fusion.76), channel_id=1, replica_groups=mesh['blk'=32,'rep'=2,'feat'=4] {'blk'}, use_global_device_ids=true, to_apply=%region_8.10 | all-reduce | flops 16384 | bytes 65536 | tf_op jit(solution)/shard_map/psum | solution.py:110
  (806 shorter events, 302.3 us)
Async XLA Ops:
  7.2 199.3 %copy-start = (bf16[64,256]{1,0:T(8,128)(2,1)S(1)}, bf16[64,256]{1,0:T(8,128)(2,1)}, u32[]{:S(2)}) copy-start(bf16[64,256]{1,0:T(8,128)(2,1)} %param.26) | copy-start | bytes 98308
  7.2 226.0 %reduce-scatter.4.cloned.1.call-start = ((), (), s32[]{:S(2)}) async-start(), calls=%async_computation.2 | async-start | bytes 655360 | tf_op jit(solution)/shard_map/reduce_scatter | solution.py:88
  7.2 14.3 %collective-permute-start.2 = (bf16[64,512]{1,0:T(8,128)(2,1)}, bf16[64,512]{1,0:T(8,128)(2,1)S(1)}, u32[]{:S(2)}, u32[]{:S(2)}) collective-permute-start(bf16[64,512]{1,0:T(8,128)(2,1)} %param.21), channel_id=1, source_target_pairs={{128,0},{136,8},{144,16},{152,24},{160,32},{168,40},{176,48},{184,... | collective-permute-start | bytes 196616 | tf_op jit(solution)/shard_map/ppermute | solution.py:12
  28.0 205.2 %copy-start.1 = (bf16[64,512]{1,0:T(8,128)(2,1)S(1)}, bf16[64,512]{1,0:T(8,128)(2,1)}, u32[]{:S(2)}) copy-start(bf16[64,512]{1,0:T(8,128)(2,1)} %param.27) | copy-start | bytes 196612
  28.0 6.6 %collective-permute-start.1 = (bf16[64,512]{1,0:T(8,128)(2,1)S(1)}, bf16[64,512]{1,0:T(8,128)(2,1)S(1)}, u32[]{:S(2)}, u32[]{:S(2)}) collective-permute-start(bf16[64,512]{1,0:T(8,128)(2,1)S(1)} %get-tuple-element.1609), channel_id=1, source_target_pairs={{248,0},{0,8},{8,16},{16,24},{24,32},{32,40},{40,48},{48,56},{56,6... | collective-permute-start | bytes 196616 | tf_op jit(solution)/shard_map/while/body/eval_jaxpr/ppermute | solution.py:12
  40.2 5.3 collective-permute-start.1
  51.0 3.4 collective-permute-start.1
  60.0 5.3 collective-permute-start.1
  69.0 8.9 %collective-permute-start.1 = (bf16[64,512]{1,0:T(8,128)(2,1)S(1)}, bf16[64,512]{1,0:T(8,128)(2,1)S(1)}, u32[]{:S(2)}, u32[]{:S(2)}) collective-permute-start(bf16[64,512]{1,0:T(8,128)(2,1)S(1)} %get-tuple-element.1609), channel_id=1, source_target_pairs={{248,0},{0,8},{8,16},{16,24},{24,32},{32,40},{40,48},{48,56},{56,6... | collective-permute-start | bytes 196616 | tf_op jit(solution)/shard_map/while/body/eval_jaxpr/ppermute | solution.py:12
  83.4 7.4 %collective-permute-start.1 = (bf16[64,512]{1,0:T(8,128)(2,1)S(1)}, bf16[64,512]{1,0:T(8,128)(2,1)S(1)}, u32[]{:S(2)}, u32[]{:S(2)}) collective-permute-start(bf16[64,512]{1,0:T(8,128)(2,1)S(1)} %get-tuple-element.1609), channel_id=1, source_target_pairs={{248,0},{0,8},{8,16},{16,24},{24,32},{32,40},{40,48},{48,56},{56,6... | collective-permute-start | bytes 196616 | tf_op jit(solution)/shard_map/while/body/eval_jaxpr/ppermute | solution.py:12
  94.6 9.2 %collective-permute-start.1 = (bf16[64,512]{1,0:T(8,128)(2,1)S(1)}, bf16[64,512]{1,0:T(8,128)(2,1)S(1)}, u32[]{:S(2)}, u32[]{:S(2)}) collective-permute-start(bf16[64,512]{1,0:T(8,128)(2,1)S(1)} %get-tuple-element.1609), channel_id=1, source_target_pairs={{248,0},{0,8},{8,16},{16,24},{24,32},{32,40},{40,48},{48,56},{56,6... | collective-permute-start | bytes 196616 | tf_op jit(solution)/shard_map/while/body/eval_jaxpr/ppermute | solution.py:12
  107.5 7.4 %collective-permute-start.1 = (bf16[64,512]{1,0:T(8,128)(2,1)S(1)}, bf16[64,512]{1,0:T(8,128)(2,1)S(1)}, u32[]{:S(2)}, u32[]{:S(2)}) collective-permute-start(bf16[64,512]{1,0:T(8,128)(2,1)S(1)} %get-tuple-element.1609), channel_id=1, source_target_pairs={{248,0},{0,8},{8,16},{16,24},{24,32},{32,40},{40,48},{48,56},{56,6... | collective-permute-start | bytes 196616 | tf_op jit(solution)/shard_map/while/body/eval_jaxpr/ppermute | solution.py:12
  120.4 5.5 collective-permute-start.1
  129.7 7.4 %collective-permute-start.1 = (bf16[64,512]{1,0:T(8,128)(2,1)S(1)}, bf16[64,512]{1,0:T(8,128)(2,1)S(1)}, u32[]{:S(2)}, u32[]{:S(2)}) collective-permute-start(bf16[64,512]{1,0:T(8,128)(2,1)S(1)} %get-tuple-element.1609), channel_id=1, source_target_pairs={{248,0},{0,8},{8,16},{16,24},{24,32},{32,40},{40,48},{48,56},{56,6... | collective-permute-start | bytes 196616 | tf_op jit(solution)/shard_map/while/body/eval_jaxpr/ppermute | solution.py:12
  142.6 5.5 collective-permute-start.1
  151.9 9.2 %collective-permute-start.1 = (bf16[64,512]{1,0:T(8,128)(2,1)S(1)}, bf16[64,512]{1,0:T(8,128)(2,1)S(1)}, u32[]{:S(2)}, u32[]{:S(2)}) collective-permute-start(bf16[64,512]{1,0:T(8,128)(2,1)S(1)} %get-tuple-element.1609), channel_id=1, source_target_pairs={{248,0},{0,8},{8,16},{16,24},{24,32},{32,40},{40,48},{48,56},{56,6... | collective-permute-start | bytes 196616 | tf_op jit(solution)/shard_map/while/body/eval_jaxpr/ppermute | solution.py:12
  166.7 5.5 collective-permute-start.1
  177.8 7.4 %collective-permute-start.1 = (bf16[64,512]{1,0:T(8,128)(2,1)S(1)}, bf16[64,512]{1,0:T(8,128)(2,1)S(1)}, u32[]{:S(2)}, u32[]{:S(2)}) collective-permute-start(bf16[64,512]{1,0:T(8,128)(2,1)S(1)} %get-tuple-element.1609), channel_id=1, source_target_pairs={{248,0},{0,8},{8,16},{16,24},{24,32},{32,40},{40,48},{48,56},{56,6... | collective-permute-start | bytes 196616 | tf_op jit(solution)/shard_map/while/body/eval_jaxpr/ppermute | solution.py:12
  188.9 7.4 %collective-permute-start.1 = (bf16[64,512]{1,0:T(8,128)(2,1)S(1)}, bf16[64,512]{1,0:T(8,128)(2,1)S(1)}, u32[]{:S(2)}, u32[]{:S(2)}) collective-permute-start(bf16[64,512]{1,0:T(8,128)(2,1)S(1)} %get-tuple-element.1609), channel_id=1, source_target_pairs={{248,0},{0,8},{8,16},{16,24},{24,32},{32,40},{40,48},{48,56},{56,6... | collective-permute-start | bytes 196616 | tf_op jit(solution)/shard_map/while/body/eval_jaxpr/ppermute | solution.py:12
  207.8 370.2 %all-reduce.3.cloned.1.call-start = ((), (), s32[]{:S(2)}) async-start(), calls=%async_computation.1 | async-start | bytes 131072 | tf_op jit(solution)/shard_map/psum | solution.py:133
  248.5 10.2 %collective-permute-start = (f32[64,512]{1,0:T(8,128)S(1)}, f32[64,512]{1,0:T(8,128)S(1)}, u32[]{:S(2)}, u32[]{:S(2)}) collective-permute-start(f32[64,512]{1,0:T(8,128)S(1)} %get-tuple-element.1699), channel_id=1, source_target_pairs={{8,0},{16,8},{24,16},{32,24},{40,32},{48,40},{56,48},{64,56},{72,6... | collective-permute-start | bytes 393224 | tf_op jit(solution)/shard_map/while/body/eval_jaxpr/ppermute | solution.py:12
  262.4 6.0 %collective-permute-start = (f32[64,512]{1,0:T(8,128)S(1)}, f32[64,512]{1,0:T(8,128)S(1)}, u32[]{:S(2)}, u32[]{:S(2)}) collective-permute-start(f32[64,512]{1,0:T(8,128)S(1)} %get-tuple-element.1699), channel_id=1, source_target_pairs={{8,0},{16,8},{24,16},{32,24},{40,32},{48,40},{56,48},{64,56},{72,6... | collective-permute-start | bytes 393224 | tf_op jit(solution)/shard_map/while/body/eval_jaxpr/ppermute | solution.py:12
  273.8 6.0 %collective-permute-start = (f32[64,512]{1,0:T(8,128)S(1)}, f32[64,512]{1,0:T(8,128)S(1)}, u32[]{:S(2)}, u32[]{:S(2)}) collective-permute-start(f32[64,512]{1,0:T(8,128)S(1)} %get-tuple-element.1699), channel_id=1, source_target_pairs={{8,0},{16,8},{24,16},{32,24},{40,32},{48,40},{56,48},{64,56},{72,6... | collective-permute-start | bytes 393224 | tf_op jit(solution)/shard_map/while/body/eval_jaxpr/ppermute | solution.py:12
  285.3 6.0 %collective-permute-start = (f32[64,512]{1,0:T(8,128)S(1)}, f32[64,512]{1,0:T(8,128)S(1)}, u32[]{:S(2)}, u32[]{:S(2)}) collective-permute-start(f32[64,512]{1,0:T(8,128)S(1)} %get-tuple-element.1699), channel_id=1, source_target_pairs={{8,0},{16,8},{24,16},{32,24},{40,32},{48,40},{56,48},{64,56},{72,6... | collective-permute-start | bytes 393224 | tf_op jit(solution)/shard_map/while/body/eval_jaxpr/ppermute | solution.py:12
  294.9 8.1 %collective-permute-start = (f32[64,512]{1,0:T(8,128)S(1)}, f32[64,512]{1,0:T(8,128)S(1)}, u32[]{:S(2)}, u32[]{:S(2)}) collective-permute-start(f32[64,512]{1,0:T(8,128)S(1)} %get-tuple-element.1699), channel_id=1, source_target_pairs={{8,0},{16,8},{24,16},{32,24},{40,32},{48,40},{56,48},{64,56},{72,6... | collective-permute-start | bytes 393224 | tf_op jit(solution)/shard_map/while/body/eval_jaxpr/ppermute | solution.py:12
  308.5 6.0 %collective-permute-start = (f32[64,512]{1,0:T(8,128)S(1)}, f32[64,512]{1,0:T(8,128)S(1)}, u32[]{:S(2)}, u32[]{:S(2)}) collective-permute-start(f32[64,512]{1,0:T(8,128)S(1)} %get-tuple-element.1699), channel_id=1, source_target_pairs={{8,0},{16,8},{24,16},{32,24},{40,32},{48,40},{56,48},{64,56},{72,6... | collective-permute-start | bytes 393224 | tf_op jit(solution)/shard_map/while/body/eval_jaxpr/ppermute | solution.py:12
  318.1 8.3 %collective-permute-start = (f32[64,512]{1,0:T(8,128)S(1)}, f32[64,512]{1,0:T(8,128)S(1)}, u32[]{:S(2)}, u32[]{:S(2)}) collective-permute-start(f32[64,512]{1,0:T(8,128)S(1)} %get-tuple-element.1699), channel_id=1, source_target_pairs={{8,0},{16,8},{24,16},{32,24},{40,32},{48,40},{56,48},{64,56},{72,6... | collective-permute-start | bytes 393224 | tf_op jit(solution)/shard_map/while/body/eval_jaxpr/ppermute | solution.py:12
  332.0 6.2 %collective-permute-start = (f32[64,512]{1,0:T(8,128)S(1)}, f32[64,512]{1,0:T(8,128)S(1)}, u32[]{:S(2)}, u32[]{:S(2)}) collective-permute-start(f32[64,512]{1,0:T(8,128)S(1)} %get-tuple-element.1699), channel_id=1, source_target_pairs={{8,0},{16,8},{24,16},{32,24},{40,32},{48,40},{56,48},{64,56},{72,6... | collective-permute-start | bytes 393224 | tf_op jit(solution)/shard_map/while/body/eval_jaxpr/ppermute | solution.py:12
  341.9 9.9 %collective-permute-start = (f32[64,512]{1,0:T(8,128)S(1)}, f32[64,512]{1,0:T(8,128)S(1)}, u32[]{:S(2)}, u32[]{:S(2)}) collective-permute-start(f32[64,512]{1,0:T(8,128)S(1)} %get-tuple-element.1699), channel_id=1, source_target_pairs={{8,0},{16,8},{24,16},{32,24},{40,32},{48,40},{56,48},{64,56},{72,6... | collective-permute-start | bytes 393224 | tf_op jit(solution)/shard_map/while/body/eval_jaxpr/ppermute | solution.py:12
  355.5 11.7 %collective-permute-start = (f32[64,512]{1,0:T(8,128)S(1)}, f32[64,512]{1,0:T(8,128)S(1)}, u32[]{:S(2)}, u32[]{:S(2)}) collective-permute-start(f32[64,512]{1,0:T(8,128)S(1)} %get-tuple-element.1699), channel_id=1, source_target_pairs={{8,0},{16,8},{24,16},{32,24},{40,32},{48,40},{56,48},{64,56},{72,6... | collective-permute-start | bytes 393224 | tf_op jit(solution)/shard_map/while/body/eval_jaxpr/ppermute | solution.py:12
  372.7 6.2 %collective-permute-start = (f32[64,512]{1,0:T(8,128)S(1)}, f32[64,512]{1,0:T(8,128)S(1)}, u32[]{:S(2)}, u32[]{:S(2)}) collective-permute-start(f32[64,512]{1,0:T(8,128)S(1)} %get-tuple-element.1699), channel_id=1, source_target_pairs={{8,0},{16,8},{24,16},{32,24},{40,32},{48,40},{56,48},{64,56},{72,6... | collective-permute-start | bytes 393224 | tf_op jit(solution)/shard_map/while/body/eval_jaxpr/ppermute | solution.py:12
  382.6 9.9 %collective-permute-start = (f32[64,512]{1,0:T(8,128)S(1)}, f32[64,512]{1,0:T(8,128)S(1)}, u32[]{:S(2)}, u32[]{:S(2)}) collective-permute-start(f32[64,512]{1,0:T(8,128)S(1)} %get-tuple-element.1699), channel_id=1, source_target_pairs={{8,0},{16,8},{24,16},{32,24},{40,32},{48,40},{56,48},{64,56},{72,6... | collective-permute-start | bytes 393224 | tf_op jit(solution)/shard_map/while/body/eval_jaxpr/ppermute | solution.py:12
  398.0 6.2 %collective-permute-start = (f32[64,512]{1,0:T(8,128)S(1)}, f32[64,512]{1,0:T(8,128)S(1)}, u32[]{:S(2)}, u32[]{:S(2)}) collective-permute-start(f32[64,512]{1,0:T(8,128)S(1)} %get-tuple-element.1699), channel_id=1, source_target_pairs={{8,0},{16,8},{24,16},{32,24},{40,32},{48,40},{56,48},{64,56},{72,6... | collective-permute-start | bytes 393224 | tf_op jit(solution)/shard_map/while/body/eval_jaxpr/ppermute | solution.py:12
  409.7 6.2 %collective-permute-start = (f32[64,512]{1,0:T(8,128)S(1)}, f32[64,512]{1,0:T(8,128)S(1)}, u32[]{:S(2)}, u32[]{:S(2)}) collective-permute-start(f32[64,512]{1,0:T(8,128)S(1)} %get-tuple-element.1699), channel_id=1, source_target_pairs={{8,0},{16,8},{24,16},{32,24},{40,32},{48,40},{56,48},{64,56},{72,6... | collective-permute-start | bytes 393224 | tf_op jit(solution)/shard_map/while/body/eval_jaxpr/ppermute | solution.py:12
  421.4 8.1 %collective-permute-start = (f32[64,512]{1,0:T(8,128)S(1)}, f32[64,512]{1,0:T(8,128)S(1)}, u32[]{:S(2)}, u32[]{:S(2)}) collective-permute-start(f32[64,512]{1,0:T(8,128)S(1)} %get-tuple-element.1699), channel_id=1, source_target_pairs={{8,0},{16,8},{24,16},{32,24},{40,32},{48,40},{56,48},{64,56},{72,6... | collective-permute-start | bytes 393224 | tf_op jit(solution)/shard_map/while/body/eval_jaxpr/ppermute | solution.py:12
  435.0 7.1 %collective-permute-start.3 = (bf16[64,512]{1,0:T(8,128)(2,1)S(1)}, bf16[64,512]{1,0:T(8,128)(2,1)S(1)}, u32[]{:S(2)}, u32[]{:S(2)}) collective-permute-start(bf16[64,512]{1,0:T(8,128)(2,1)S(1)} %convert_element_type.73), channel_id=1, source_target_pairs={{128,0},{136,8},{144,16},{152,24},{160,32},{168,40},{176,48},{184,... | collective-permute-start | bytes 196616 | tf_op jit(solution)/shard_map/ppermute | solution.py:12
Sparse Core Ops, SparseCore 0:
  207.9 25.2 reduce-scatter.3
  442.9 34.9 all-reduce.2
where the time goes:
time: 592 us; the launch traced here: 586 us
  blocking collectives  151 us (26%)
  local copies, waits for them, and re-layouts  130 us (22%)
  starting transfers between devices  84.2 us (14%)
  waiting for transfers between devices  82.9 us (14%)
  other arithmetic  64.5 us (11%)
  matrix products  32.6 us (6%)
  loops' own time  25.6 us (4%)
  between operations  15.5 us (3%)
    psum x1, blocking collectives, body(): lax.psum((weight_part * node_scale).astype(jnp.bfloat16), 'blk')  134 us
    ppermute x32, starting transfers between devices, passed_along(): return lax.ppermute(block, axis, route)  84.1 us
    ppermute x32, waiting for transfers between devices, passed_along(): return lax.ppermute(block, axis, route)  58.2 us
    and x82, other arithmetic, one_turn(): chosen = jnp.take(source, pick_group, axis=1)  57.4 us
    gather x82, local copies, waits for them, and re-layouts, one_turn(): chosen = jnp.take(source, pick_group, axis=1)  46.2 us
    dynamic_slice x31, local copies, waits for them, and re-layouts, section_arrays(): lax.dynamic_index_in_dim(counts, section, 0, False)  38.9 us
    squeeze x31, local copies, waits for them, and re-layouts, section_arrays(): lax.dynamic_index_in_dim(tile_set, section, 0, False)  32 us
    reduce_scatter x1, waiting for transfers between devices, body(): lax.psum_scatter(lax.dot_general(columns, aggregated, (((0,), (0,)), ((),...  24.7 us
  transfers between devices with their start and end apart: 34, of which 18 were waited for; matrix products, arithmetic and copies ran while one was open for 13% of the time, Pallas kernels for 0%

commit v1 on v0

v1 whole, which is shorter than its diff:
```python
import jax
import jax.numpy as jnp
from jax import lax
from jax.experimental import pallas as pl
from jax.experimental.pallas import tpu as pltpu
from jax.sharding import PartitionSpec as P

MESH = pl.DeviceIdType.MESH
BF16, F32 = jnp.bfloat16, jnp.float32
RING = 8
SIDE = 4
SLOTS = 12
TILE = 128
ROWS = 64
NODES = 512
PARTS = 32
HALF = ROWS // 2

ORDER = [(d, cc) for d in (0, 1, 7, 2, 6, 3, 5, 4) for cc in (0, 1)]
PLACE = {pair: n for n, pair in enumerate(ORDER)}


def kernel(
    feat, tiles, tile_rows, tile_cols, tile_count, weight, cot,
    hid, wgrad, igrad,
    raw, acc, dense, panels, agg, w_all, w_turned, cot_all,
    agg_out, agg_in, hid_out, sig_out, sig_in,
    g1_out, g1, g2_out, g2, g3_out, g3, g4_out,
    back_out, back_in, keep, chain_out, chain_in, fin_out, fin_in, done,
    tile_sem, local_sem, hop_sem, ring_send, ring_recv, core_send, core_recv,
    w_send, w_recv, cot_send, cot_recv, agg_send, agg_recv, sig_send, sig_recv,
    hid_send, hid_recv, g1_send, g1_recv, g2_send, g2_recv, g3_send, g3_recv, g4_send, g4_recv,
    back_send, back_recv, chain_send, chain_recv, fin_send, fin_recv,
):
    p, r, f = lax.axis_index("blk"), lax.axis_index("rep"), lax.axis_index("feat")
    z, xh, c = p // 4, (p // 2) % 2, p % 2

    def at(dz=0, dx=0, dc=0, dr=0, df=0):
        nz = (z + dz) % RING
        nx, nc, nr = (xh + dx) % 2, (c + dc) % 2, (r + dr) % 2
        return (nz * 4 + nx * 2 + nc, nr, (f + df) % SIDE)

    def remote(src, dst, send, recv, device):
        return pltpu.make_async_remote_copy(
            src_ref=src, dst_ref=dst, send_sem=send, recv_sem=recv, device_id=device, device_id_type=MESH
        )

    def tile_copy(n):
        half = n // 2
        odd, step = half % 2, (half + 1) // 2
        d = (odd * step + (1 - odd) * (RING - step)) % RING
        source = ((z + RING - d) % RING) * 4 + ((xh + r) % 2) * 2 + (c + n % 2) % 2
        section = (p + PARTS - source) % PARTS
        return section, pltpu.make_async_copy(tiles.at[0, section], raw.at[n], tile_sem.at[n])

    own_feat = pltpu.make_async_copy(feat, panels.at[0, 0], local_sem.at[0])
    own_w = pltpu.make_async_copy(weight, w_all.at[f], local_sem.at[1])
    own_lanes = pl.ds(pl.multiple_of(f * TILE, TILE), TILE)
    own_cot = pltpu.make_async_copy(cot.at[:, own_lanes], cot_all.at[f], local_sem.at[2])

    @pl.when(r == 0)
    def _():
        own_feat.start()

    own_w.start()
    own_cot.start()

    def start_tiles(n, carried):
        tile_copy(n)[1].start()
        return carried

    lax.fori_loop(0, 16, start_tiles, 0)

    partners = [at(dz=dz) for dz in range(1, RING)]
    partners += [at(dx=i // 4, dc=(i // 2) % 2, dr=i % 2) for i in range(1, 8)]
    partners += [at(dr=dr, df=df) for dr in range(2) for df in range(1, SIDE)]
    barrier = pltpu.get_barrier_semaphore()
    for device in partners:
        pl.semaphore_signal(barrier, inc=1, device_id=device, device_id_type=MESH)
    acc[SLOTS] = jnp.zeros((TILE, TILE), BF16)
    agg[...] = jnp.zeros_like(agg)
    pl.semaphore_wait(barrier, len(partners))

    hop = remote(panels.at[0, 0], panels.at[0, 0], hop_sem.at[0], hop_sem.at[1], at(dx=1, dr=1))

    @pl.when(r == 0)
    def _():
        own_feat.wait()
        hop.start()

    @pl.when(r == 1)
    def _():
        hop.wait_recv()

    def ring_copy(way, step, chunk):
        d = step if way == 0 else (RING - step) % RING
        to = d + 1 if way == 0 else RING - 1 - step
        span = pl.ds(chunk * HALF, HALF)
        return remote(
            panels.at[d, 0, span], panels.at[to, 0, span],
            ring_send.at[way, step, chunk], ring_recv.at[way, step, chunk],
            at(dz=1 if way == 0 else RING - 1),
        )

    def core_copy(d):
        return remote(panels.at[d, 0], panels.at[d, 1], core_send.at[d], core_recv.at[d], at(dc=1))

    for chunk in range(2):
        for way in range(2):
            ring_copy(way, 0, chunk).start()
    core_copy(0).start()

    def w_copy(df):
        return remote(weight, w_all.at[f], w_send.at[df], w_recv.at[df], at(df=df))

    def cot_copy(df):
        lanes = pl.ds(pl.multiple_of(((f + df) % SIDE) * TILE, TILE), TILE)
        return remote(cot.at[:, lanes], cot_all.at[f], cot_send.at[df], cot_recv.at[df], at(df=df))

    for df in range(1, SIDE):
        w_copy(df).start()
        cot_copy(df).start()

    def densify(n, carried):
        section, copy = tile_copy(n)
        copy.wait()
        live = tile_count[0, section]
        target = [
            jnp.where(t < live, tile_rows[0, section, t] * SIDE + tile_cols[0, section, t], 16)
            for t in range(SLOTS)
        ]
        for t in range(SLOTS):
            before = jnp.int32(SLOTS)
            for u in range(t):
                before = jnp.where(target[u] == target[t], u, before)
            acc[t] = raw[n, t] + acc[before]
        for b in range(16):
            last = jnp.int32(SLOTS)
            for t in range(SLOTS):
                last = jnp.where(target[t] == b, t, last)
            i, j = b // SIDE, b % SIDE
            dense[n, i * TILE:(i + 1) * TILE, j * TILE:(j + 1) * TILE] = acc[last]
        return carried

    def forward(d, cc):
        if cc:
            core_copy(d).wait_recv()
        agg[...] += lax.dot_general(
            panels[d, cc], dense[PLACE[d, cc]], (((1,), (1,)), ((), ())), preferred_element_type=F32
        )

    lax.fori_loop(0, 4, densify, 0)
    for step in range(4):
        for chunk in range(2):
            for way in range(2):
                if step < 3 or chunk == way:
                    ring_copy(way, step, chunk).wait_recv()
                    if step < 2 or (step == 2 and chunk == way):
                        ring_copy(way, step + 1, chunk).start()
        core_copy(step + 1).start()
        if step < 3:
            core_copy(RING - 1 - step).start()
            lax.fori_loop(4 * step + 4, 4 * step + 8, densify, 0)
        if step == 0:
            forward(0, 0)
            forward(0, 1)
        else:
            for d in (step, RING - step):
                forward(d, 0)
                forward(d, 1)
        if step == 2:
            own_w.wait()
            for df in range(1, SIDE):
                w_copy(df).wait_recv()
            w_turned[...] = w_all[...].reshape(256, 256).astype(F32).T.astype(BF16)
    forward(4, 0)
    forward(4, 1)

    def agg_copy(dr, df):
        return remote(
            agg_out.at[(f + df) % SIDE], agg_in.at[r, f], agg_send.at[dr, df], agg_recv.at[dr, df], at(dr=dr, df=df)
        )

    group = [(dr, df) for df in (2, 1, 3, 0) for dr in (1, 0) if dr or df]
    for b in range(SIDE):
        agg_out[b] = agg[:, b * TILE:(b + 1) * TILE].astype(BF16)
    for dr, df in group:
        agg_copy(dr, df).start()
    agg_in[r, f] = agg_out[f]
    own_cot.wait()
    for df in range(1, SIDE):
        cot_copy(df).wait_recv()
    for dr, df in group:
        agg_copy(dr, df).wait_recv()
    summed = (agg_in[0].astype(F32) + agg_in[1].astype(F32)).reshape(256, TILE).astype(BF16)
    pre_act = jnp.dot(w_turned[...], summed, preferred_element_type=F32)
    gate = 1.0 / (1.0 + jnp.exp(-pre_act))
    grad = cot_all[...].reshape(256, TILE).astype(F32)
    pre_grad = (grad * gate * (1.0 + pre_act * (1.0 - gate))).astype(BF16)
    signal = jnp.dot(w_all[...].reshape(256, 256), pre_grad, preferred_element_type=F32)
    sig_out[...] = signal.astype(BF16).reshape(SIDE, ROWS, TILE)

    def sig_copy(df):
        return remote(sig_out.at[(f + df) % SIDE], sig_in.at[f], sig_send.at[df], sig_recv.at[df], at(df=df))

    for df in (2, 1, 3):
        sig_copy(df).start()
    sig_in[f] = sig_out[f]

    hid_out[...] = (pre_act * gate).astype(BF16).reshape(SIDE, ROWS, TILE)

    def hid_copy(df):
        return remote(
            hid_out.at[(f + df) % SIDE], hid.at[:, own_lanes], hid_send.at[df], hid_recv.at[df], at(df=df)
        )

    own_hid = pltpu.make_async_copy(hid_out.at[f], hid.at[:, own_lanes], local_sem.at[3])
    own_hid.start()
    for df in range(1, SIDE):
        hid_copy(df).start()
    grad_rows = jnp.where(r == 0, pre_grad[:TILE].astype(F32), pre_grad[TILE:].astype(F32)).astype(BF16)
    share = lax.dot_general(summed, grad_rows, (((1,), (1,)), ((), ())), preferred_element_type=F32)
    g1_out[...] = share.reshape(SIDE, ROWS, TILE)

    def g1_copy(df):
        return remote(g1_out.at[(f + df) % SIDE], g1.at[f], g1_send.at[df], g1_recv.at[df], at(df=df))

    for df in range(1, SIDE):
        g1_copy(df).start()
    g1[f] = g1_out[f]

    for df in (2, 1, 3):
        sig_copy(df).wait_recv()
    signal_row = jnp.concatenate([sig_in[b] for b in range(SIDE)], axis=1)

    def backward(d, cc):
        return jnp.dot(signal_row, dense[PLACE[d, cc]], preferred_element_type=F32)

    def back_copy(d):
        return remote(back_out.at[d], back_in.at[d], back_send.at[d], back_recv.at[d], at(dc=1))

    def give(d):
        back_out[d] = backward(d, 1).astype(BF16)
        back_copy(d).start()

    def take(d):
        keep[d] = backward(d, 0)
        back_copy(d).wait_recv()
        keep[d] += back_in[d].astype(F32)

    def chain_copy(way, level, chunk):
        span = pl.ds(chunk * HALF, HALF)
        return remote(
            chain_out.at[way, level - 1, span], chain_in.at[way, level - 1, span],
            chain_send.at[way, level - 1, chunk], chain_recv.at[way, level - 1, chunk],
            at(dz=RING - 1 if way == 0 else 1),
        )

    def pass_on(way, level, chunk):
        d = level if way == 0 else RING - level
        rows = slice(chunk * HALF, (chunk + 1) * HALF)
        value = keep[d, rows]
        if level < 3 or (level == 3 and chunk != way):
            chain_copy(way, level + 1, chunk).wait_recv()
            value = value + chain_in[way, level, rows].astype(F32)
        chain_out[way, level - 1, rows] = value.astype(BF16)
        chain_copy(way, level, chunk).start()

    give(4)
    give(3)
    give(5)
    take(4)
    pass_on(0, 4, 1)
    pass_on(1, 4, 0)
    give(2)
    give(6)
    take(3)
    pass_on(0, 3, 0)
    take(5)
    pass_on(1, 3, 1)
    pass_on(0, 3, 1)
    pass_on(1, 3, 0)

    for df in range(1, SIDE):
        g1_copy(df).wait_recv()
    g2_out[...] = (g1[0] + g1[1]) + (g1[2] + g1[3])

    def g2_copy(dz):
        rows = pl.ds(pl.multiple_of(((z + dz) % RING) * 8, 8), 8)
        return remote(g2_out.at[rows], g2.at[z], g2_send.at[dz], g2_recv.at[dz], at(dz=dz))

    for dz in range(1, RING):
        g2_copy(dz).start()
    g2[z] = g2_out[pl.ds(pl.multiple_of(z * 8, 8), 8)]

    give(1)
    give(7)
    take(2)
    take(6)
    for chunk in range(2):
        pass_on(0, 2, chunk)
        pass_on(1, 2, 1 - chunk)

    for dz in range(1, RING):
        g2_copy(dz).wait_recv()
    g3_out[...] = jnp.sum(g2[...], axis=0)

    def g3_copy(i):
        return remote(
            g3_out, g3.at[r * 4 + xh * 2 + c], g3_send.at[i], g3_recv.at[i],
            at(dx=i // 4, dc=(i // 2) % 2, dr=i % 2),
        )

    for i in range(1, 8):
        g3_copy(i).start()
    g3[r * 4 + xh * 2 + c] = g3_out[...]

    give(0)
    take(1)
    take(7)
    for chunk in range(2):
        pass_on(0, 1, chunk)
        pass_on(1, 1, 1 - chunk)

    for i in range(1, 8):
        g3_copy(i).wait_recv()
    scale = float(NODES * PARTS) ** -0.5
    for half in range(2):
        four = (g3[4 * half] + g3[4 * half + 1]) + (g3[4 * half + 2] + g3[4 * half + 3])
        g4_out[:, half * TILE:(half + 1) * TILE] = four * scale
    own_rows = pl.ds(pl.multiple_of(z * 8, 8), 8)

    def g4_copy(dz):
        return remote(g4_out, wgrad.at[own_rows], g4_send.at[dz], g4_recv.at[dz], at(dz=dz))

    for dz in range(1, RING):
        g4_copy(dz).start()
    own_wgrad = pltpu.make_async_copy(g4_out, wgrad.at[own_rows], local_sem.at[4])
    own_wgrad.start()

    take(0)

    def fin_copy(i, chunk):
        span = pl.ds(chunk * HALF, HALF)
        device = (at(dr=1), at(dx=1, dr=1), at(dx=1))[i]
        return remote(
            fin_out.at[span], fin_in.at[min(i, 1), span], fin_send.at[i, chunk], fin_recv.at[min(i, 1), chunk], device
        )

    for chunk in range(2):
        rows = slice(chunk * HALF, (chunk + 1) * HALF)
        value = keep[0, rows]
        for way in range(2):
            chain_copy(way, 1, chunk).wait_recv()
            value = value + chain_in[way, 0, rows].astype(F32)
        fin_out[rows] = value.astype(BF16)

        @pl.when(r == 0)
        def _():
            fin_copy(0, chunk).start()

        @pl.when(r == 1)
        def _():
            fin_copy(2, chunk).start()
            fin_copy(1, chunk).start()

    for chunk in range(2):
        rows = slice(chunk * HALF, (chunk + 1) * HALF)
        fin_copy(1, chunk).wait_recv()

        @pl.when(r == 0)
        def _():
            fin_in[0, rows] = fin_out[rows]

        @pl.when(r == 1)
        def _():
            fin_copy(0, chunk).wait_recv()

        done[rows] = (fin_in[0, rows].astype(F32) + fin_in[1, rows].astype(F32)).astype(BF16)
    own_igrad = pltpu.make_async_copy(done, igrad, local_sem.at[5])
    own_igrad.start()

    @pl.when(r == 0)
    def _():
        hop.wait_send()
        for chunk in range(2):
            fin_copy(0, chunk).wait_send()

    @pl.when(r == 1)
    def _():
        for chunk in range(2):
            fin_copy(1, chunk).wait_send()
            fin_copy(2, chunk).wait_send()

    for way in range(2):
        for step in range(4):
            for chunk in range(2):
                if step < 3 or chunk == way:
                    ring_copy(way, step, chunk).wait_send()
        for level in range(1, 5):
            for chunk in range(2):
                if level < 4 or chunk != way:
                    chain_copy(way, level, chunk).wait_send()
    for d in range(RING):
        core_copy(d).wait_send()
        back_copy(d).wait_send()
    for dr, df in group:
        agg_copy(dr, df).wait_send()
    for df in range(1, SIDE):
        w_copy(df).wait_send()
        cot_copy(df).wait_send()
        sig_copy(df).wait_send()
        g1_copy(df).wait_send()
        hid_copy(df).wait()
    for dz in range(1, RING):
        g2_copy(dz).wait_send()
        g3_copy(dz).wait_send()
        g4_copy(dz).wait()
    own_hid.wait()
    own_wgrad.wait()
    own_igrad.wait()


def body(features_t, tile_values, tile_rows, tile_cols, tile_count, weight, cotangent_t):
    anywhere = pl.BlockSpec(memory_space=pl.ANY)
    scalars = pl.BlockSpec(memory_space=pltpu.SMEM)
    vmem, dma = pltpu.VMEM, pltpu.SemaphoreType.DMA
    block = (SIDE, ROWS, TILE)
    panel = (ROWS, NODES)
    return pl.pallas_call(
        kernel,
        out_shape=(
            jax.ShapeDtypeStruct((ROWS, NODES), BF16),
            jax.ShapeDtypeStruct((ROWS, 256), F32),
            jax.ShapeDtypeStruct((ROWS, NODES), BF16),
        ),
        in_specs=[anywhere, anywhere, scalars, scalars, scalars, anywhere, anywhere],
        out_specs=(anywhere, anywhere, anywhere),
        scratch_shapes=[
            vmem((16, SLOTS, TILE, TILE), BF16),
            vmem((SLOTS + 1, TILE, TILE), BF16),
            vmem((16, NODES, NODES), BF16),
            vmem((RING, 2, *panel), BF16),
            vmem(panel, F32),
            vmem((SIDE, ROWS, 256), BF16),
            vmem((256, 256), BF16),
            vmem(block, BF16),
            vmem(block, BF16),
            vmem((2, *block), BF16),
            vmem(block, BF16),
            vmem(block, BF16),
            vmem(block, BF16),
            vmem(block, F32),
            vmem(block, F32),
            vmem((ROWS, TILE), F32),
            vmem((RING, 8, TILE), F32),
            vmem((8, TILE), F32),
            vmem((8, 8, TILE), F32),
            vmem((8, 256), F32),
            vmem((RING, *panel), BF16),
            vmem((RING, *panel), BF16),
            vmem((RING, *panel), F32),
            vmem((2, 4, *panel), BF16),
            vmem((2, 4, *panel), BF16),
            vmem(panel, BF16),
            vmem((2, *panel), BF16),
            vmem(panel, BF16),
            dma((16,)), dma((6,)), dma((2,)),
            dma((2, 4, 2)), dma((2, 4, 2)), dma((RING,)), dma((RING,)),
            dma((SIDE,)), dma((SIDE,)), dma((SIDE,)), dma((SIDE,)),
            dma((2, SIDE)), dma((2, SIDE)), dma((SIDE,)), dma((SIDE,)),
            dma((SIDE,)), dma((SIDE,)), dma((SIDE,)), dma((SIDE,)),
            dma((RING,)), dma((RING,)), dma((8,)), dma((8,)), dma((RING,)), dma((RING,)),
            dma((RING,)), dma((RING,)), dma((2, 4, 2)), dma((2, 4, 2)), dma((3, 2)), dma((2, 2)),
        ],
        compiler_params=pltpu.CompilerParams(
            collective_id=0, has_side_effects=True, vmem_limit_bytes=40 * 1024 * 1024
        ),
    )(features_t, tile_values, tile_rows, tile_cols, tile_count, weight, cotangent_t)


def solution(mesh):
    return jax.shard_map(
        body,
        mesh=mesh,
        in_specs=(
            P("feat", "blk"),
            P("blk", None, None, None, None),
            P("blk", None, None),
            P("blk", None, None),
            P("blk", None),
            P("feat", None),
            P("feat", "blk"),
        ),
        out_specs=(P("feat", "blk"), P("feat", None), P("feat", "blk")),
        check_vma=False,
    )
```

time: 592 us -> 74.8 us (0.13)
  blocking collectives: 151 us -> 0 us
  local copies, waits for them, and re-layouts: 130 us -> 11.1 us
  starting transfers between devices: 84.2 us -> 0 us
  waiting for transfers between devices: 82.9 us -> 0 us
  other arithmetic: 64.5 us -> 0 us
  Pallas kernels: 0 us -> 62.7 us
  matrix products: 32.6 us -> 0 us
  loops' own time: 25.6 us -> 0 us
  between operations: 15.5 us -> 0.65 us
    psum x2 -> x0, blocking collectives: 141 us -> none  [the longest x1 134 us: body(): lax.psum((weight_part * node_scale).astype(jnp.bfloat16), 'blk')]
    ppermute x32 -> x0, starting transfers between devices: 84.1 us -> none  [passed_along(): return lax.ppermute(block, axis, route)]
    pallas_call x0 -> x1, Pallas kernels: none -> 62.7 us  [body(): pl.pallas_call(kernel, out_shape=(jax.ShapeDtypeStruct((ROWS, NODES), BF1...]
    ppermute x32 -> x0, waiting for transfers between devices: 58.2 us -> none  [passed_along(): return lax.ppermute(block, axis, route)]
    and x82 -> x0, other arithmetic: 57.4 us -> none  [one_turn(): chosen = jnp.take(source, pick_group, axis=1)]
    dynamic_slice x114 -> x0, local copies, waits for them, and re-layouts: 47.2 us -> none  [the longest x31 38.9 us: section_arrays(): lax.dynamic_index_in_dim(counts, section, 0, False)]
    gather x82 -> x0, local copies, waits for them, and re-layouts: 46.2 us -> none  [one_turn(): chosen = jnp.take(source, pick_group, axis=1)]
    dot_general x167 -> x0, matrix products: 32.6 us -> none  [the longest x82 13.4 us: one_turn(): jnp.einsum('gb,gfi->fbi', spread, products).reshape(carried.shape)]
  transfers between devices with their start and end apart: 34 -> 0, of which waited for: 18 -> 0; matrix products, arithmetic and copies ran while one was open for 13% -> 0% of each run, Pallas kernels for 0% -> 0%
where the time goes in v1:
time: 74.8 us; the launch traced here: 74.5 us
  Pallas kernels  62.7 us (84%)
  local copies, waits for them, and re-layouts  11.1 us (15%)
    pallas_call x1, Pallas kernels, body(): pl.pallas_call(kernel, out_shape=(jax.ShapeDtypeStruct((ROWS, NODES), BF1...  62.7 us
    unnamed x15, local copies, waits for them, and re-layouts  11.1 us

profile of v1, /device:TPU:1, one launch (start us, length us, event | category | flops | bytes accessed | tf_op | source)
XLA Modules:
  0.0 74.5 jit_solution(6972479746720614151)
XLA Ops:
  0.6 0.8 %copy.10.tile_rows = s32[1,32,12]{2,1,0:T(8,128)S(1)} copy(s32[1,32,12]{1,0,2:T(1,128)} %param.9) | data formatting | bytes 3072 | tf_op args[2]
  1.4 0.8 %copy.11.tile_cols = s32[1,32,12]{2,1,0:T(8,128)S(1)} copy(s32[1,32,12]{1,0,2:T(1,128)} %param.10) | data formatting | bytes 3072 | tf_op args[3]
  2.2 0.0 copy-start
  2.2 4.6 %copy-done = bf16[1,32,12,128,128]{4,3,2,1,0:T(8,128)(2,1)S(1)} copy-done((bf16[1,32,12,128,128]{4,3,2,1,0:T(8,128)(2,1)S(1)}, bf16[1,32,12,128,128]{4,3,2,1,0:T(8,128)(2,1)}, u32[]{:S(2)}) %copy-start) | copy-done | bytes 12582936
  6.7 0.0 copy-start.1
  6.7 0.8 %copy-done.1 = bf16[64,512]{1,0:T(8,128)(2,1)S(1)} copy-done((bf16[64,512]{1,0:T(8,128)(2,1)S(1)}, bf16[64,512]{1,0:T(8,128)(2,1)}, u32[]{:S(2)}) %copy-start.1) | copy-done | bytes 65560
  7.6 0.0 copy-start.2
  7.6 0.8 %copy-done.2 = bf16[64,512]{1,0:T(8,128)(2,1)S(1)} copy-done((bf16[64,512]{1,0:T(8,128)(2,1)S(1)}, bf16[64,512]{1,0:T(8,128)(2,1)}, u32[]{:S(2)}) %copy-start.2) | copy-done | bytes 65560
  8.4 0.0 copy-start.3
  8.4 0.8 %copy-done.3 = bf16[64,256]{1,0:T(8,128)(2,1)S(1)} copy-done((bf16[64,256]{1,0:T(8,128)(2,1)S(1)}, bf16[64,256]{1,0:T(8,128)(2,1)}, u32[]{:S(2)}) %copy-start.3) | copy-done | bytes 32792
  9.2 0.0 copy-start.4
  9.2 0.7 copy-done.4
  9.8 62.7 %shard_map.94 = (bf16[64,512]{1,0:T(8,128)(2,1)S(1)}, f32[64,256]{1,0:T(8,128)S(1)}, bf16[64,512]{1,0:T(8,128)(2,1)S(1)}) custom-call(bf16[64,512]{1,0:T(8,128)(2,1)S(1)} %copy-done.1, bf16[1,32,12,128,128]{4,3,2,1,0:T(8,128)(2,1)S(1)} %copy-done, s32[1,32,12]{2,1,0:T(8,128)S(1)} %copy.10.tile_rows, s32[1,32,12]{2,1,0:T(8,128)S(1)} %copy.11.tile_cols, ...), custom_call_target="tpu_custom_call" | custom-call | tf_op jit(solution)/shard_map/pallas_call | solution.py:430
  72.6 0.6 copy.15
  73.2 0.6 copy.16
  73.8 0.6 copy.17
Async XLA Ops:
  2.2 4.6 %copy-start = (bf16[1,32,12,128,128]{4,3,2,1,0:T(8,128)(2,1)S(1)}, bf16[1,32,12,128,128]{4,3,2,1,0:T(8,128)(2,1)}, u32[]{:S(2)}) copy-start(bf16[1,32,12,128,128]{4,3,2,1,0:T(8,128)(2,1)} %tiles.1) | copy-start | bytes 37748740
  6.7 0.8 %copy-start.1 = (bf16[64,512]{1,0:T(8,128)(2,1)S(1)}, bf16[64,512]{1,0:T(8,128)(2,1)}, u32[]{:S(2)}) copy-start(bf16[64,512]{1,0:T(8,128)(2,1)} %feat.1) | copy-start | bytes 196612
  7.6 0.8 %copy-start.2 = (bf16[64,512]{1,0:T(8,128)(2,1)S(1)}, bf16[64,512]{1,0:T(8,128)(2,1)}, u32[]{:S(2)}) copy-start(bf16[64,512]{1,0:T(8,128)(2,1)} %cot.1) | copy-start | bytes 196612
  8.4 0.8 %copy-start.3 = (bf16[64,256]{1,0:T(8,128)(2,1)S(1)}, bf16[64,256]{1,0:T(8,128)(2,1)}, u32[]{:S(2)}) copy-start(bf16[64,256]{1,0:T(8,128)(2,1)} %weight.1) | copy-start | bytes 98308
  9.2 0.7 copy-start.4

commit v2 on v1

v2 whole, which is shorter than its diff:
```python
import jax
import jax.numpy as jnp
from jax import lax
from jax.experimental import pallas as pl
from jax.experimental.pallas import tpu as pltpu
from jax.sharding import PartitionSpec as P

MESH = pl.DeviceIdType.MESH
BF16, F32 = jnp.bfloat16, jnp.float32
RING = 8
SIDE = 4
SLOTS = 12
TILE = 128
ROWS = 64
NODES = 512
PARTS = 32
HALF = ROWS // 2
VMEM_BYTES = 62 * 1024 * 1024

ORDER = [(d, cc) for d in (0, 1, 7, 2, 6, 3, 5, 4) for cc in (0, 1)]
PLACE = {pair: n for n, pair in enumerate(ORDER)}
DIRECT = {2: 0, 6: 1, 1: 2, 7: 3, 0: 4}


def kernel(
    feat, tiles, rows_hbm, cols_hbm, count_hbm, weight, cot,
    hid, wgrad, igrad,
    tile_rows, tile_cols, tile_count,
    raw, acc, dense, panels, agg, w_all, w_turned, cot_all,
    agg_out, agg_in, hid_out, sig_out, sig_in,
    g1_out, g1, g2_out, g2, g3_out, g3, g4_out,
    back_out, back_in, keep, near_out, near_in, root_out, root_in, done,
    tile_sem, local_sem, first_send, first_recv, second_send, second_recv, core_send, core_recv,
    w_send, w_recv, cot_send, cot_recv, agg_send, agg_recv, sig_send, sig_recv,
    hid_send, hid_recv, g1_send, g1_recv, g2_send, g2_recv, g3_send, g3_recv, g4_send, g4_recv,
    back_send, back_recv, near_send, near_recv, root_send, root_recv, fin_send, fin_recv,
):
    p, r, f = lax.axis_index("blk"), lax.axis_index("rep"), lax.axis_index("feat")
    z, xh, c = p // 4, (p // 2) % 2, p % 2
    lane = (c + r) % 2

    def at(dz=0, dx=0, dc=0, dr=0, df=0):
        nz = (z + dz) % RING
        nx, nc, nr = (xh + dx) % 2, (c + dc) % 2, (r + dr) % 2
        return (nz * 4 + nx * 2 + nc, nr, (f + df) % SIDE)

    pending = []

    def go(copy):
        copy.start()
        pending.append(copy)

    def remote(src, dst, send, recv, device):
        return pltpu.make_async_remote_copy(
            src_ref=src, dst_ref=dst, send_sem=send, recv_sem=recv, device_id=device, device_id_type=MESH
        )

    def tile_copy(n):
        half = n // 2
        odd, step = half % 2, (half + 1) // 2
        d = (odd * step + (1 - odd) * (RING - step)) % RING
        source = ((z + RING - d) % RING) * 4 + ((xh + lane + n % 2) % 2) * 2 + r
        section = (p + PARTS - source) % PARTS
        return section, pltpu.make_async_copy(tiles.at[0, section], raw.at[n], tile_sem.at[n])

    own_feat = pltpu.make_async_copy(feat, panels.at[0, 0], local_sem.at[0])
    own_w = pltpu.make_async_copy(weight, w_all.at[f], local_sem.at[1])
    own_lanes = pl.ds(pl.multiple_of(f * TILE, TILE), TILE)
    own_cot = pltpu.make_async_copy(cot.at[:, own_lanes], cot_all.at[f], local_sem.at[2])

    scalar_copies = [
        pltpu.make_async_copy(src, dst, local_sem.at[3 + i])
        for i, (src, dst) in enumerate(((rows_hbm, tile_rows), (cols_hbm, tile_cols), (count_hbm, tile_count)))
    ]
    for copy in scalar_copies:
        copy.start()

    @pl.when(lane == 0)
    def _():
        own_feat.start()

    own_w.start()
    own_cot.start()

    def start_tiles(n, carried):
        tile_copy(n)[1].start()
        return carried

    lax.fori_loop(0, 16, start_tiles, 0)

    partners = [at(dz=dz) for dz in (4, 3, 5, 2, 6, 1, 7)]
    partners += [at(dz=dz, dx=1, dc=1) for dz in (2, 6, 1, 7, 0)]
    partners += [at(dr=dr, df=df) for df in (2, 1, 3, 0) for dr in range(2) if dr or df]
    partners += [at(dc=1), at(dx=1), at(dx=1, dr=1), at(dc=1, dr=1), at(dx=1, dc=1, dr=1)]
    barrier = pltpu.get_barrier_semaphore()
    for device in partners:
        pl.semaphore_signal(barrier, inc=1, device_id=device, device_id_type=MESH)
    acc[SLOTS] = jnp.zeros((TILE, TILE), BF16)
    agg[...] = jnp.zeros_like(agg)
    pl.semaphore_wait(barrier, len(partners))

    def first_copy(to_lane, d, chunk):
        span = pl.ds(chunk * HALF, HALF) if d in (2, 6) else pl.ds(0, ROWS)
        return remote(
            feat.at[span], panels.at[d, 0, span],
            first_send.at[to_lane, DIRECT[d], chunk], first_recv.at[DIRECT[d], chunk],
            at(dz=d, dx=to_lane, dc=to_lane),
        )

    firsts = [(to_lane, d, i ^ (d == 6)) for i in range(2) for d in (2, 6) for to_lane in (1, 0)]
    firsts += [(to_lane, d, 0) for d in (1, 7) for to_lane in (1, 0)] + [(1, 0, 0)]

    @pl.when(lane == 0)
    def _():
        for first in firsts:
            first_copy(*first).start()

    def second_copy(way, part):
        d = 2 if way == 0 else RING - 2
        step = 2 if part == 2 else 1
        to = d + step if way == 0 else d - step
        chunk = part if part < 2 else way
        span = pl.ds(chunk * HALF, HALF)
        return remote(
            panels.at[d, 0, span], panels.at[to, 0, span],
            second_send.at[way, part], second_recv.at[way, part], at(dz=step if way == 0 else RING - step),
        )

    def core_copy(d):
        return remote(panels.at[d, 0], panels.at[d, 1], core_send.at[d], core_recv.at[d], at(dc=1))

    def w_copy(df):
        return remote(weight, w_all.at[f], w_send.at[df], w_recv.at[df], at(df=df))

    def cot_copy(df):
        lanes = pl.ds(pl.multiple_of(((f + df) % SIDE) * TILE, TILE), TILE)
        return remote(cot.at[:, lanes], cot_all.at[f], cot_send.at[df], cot_recv.at[df], at(df=df))

    for df in range(1, SIDE):
        go(w_copy(df))
        go(cot_copy(df))

    def densify(n, carried):
        section, copy = tile_copy(n)
        copy.wait()
        live = tile_count[0, section]
        target = [
            jnp.where(t < live, tile_rows[t, 0, section] * SIDE + tile_cols[t, 0, section], 16)
            for t in range(SLOTS)
        ]
        for t in range(SLOTS):
            before = jnp.int32(SLOTS)
            for u in range(t):
                before = jnp.where(target[u] == target[t], u, before)
            acc[t] = raw[n, t] + acc[before]
        for b in range(16):
            last = jnp.int32(SLOTS)
            for t in range(SLOTS):
                last = jnp.where(target[t] == b, t, last)
            i, j = b // SIDE, b % SIDE
            dense[n, i * TILE:(i + 1) * TILE, j * TILE:(j + 1) * TILE] = acc[last]
        return carried

    def forward(d, cc):
        if cc:
            core_copy(d).wait_recv()
        agg[...] += lax.dot_general(
            panels[d, cc], dense[PLACE[d, cc]], (((1,), (1,)), ((), ())), preferred_element_type=F32
        )

    for copy in scalar_copies:
        copy.wait()
    lax.fori_loop(0, 16, densify, 0)
    for i in range(2):
        for way in range(2):
            chunk = i ^ way
            first_copy(0, 2 if way == 0 else 6, chunk).wait_recv()
            if i == 0:
                go(second_copy(way, 2))
            go(second_copy(way, chunk))
    go(core_copy(2))
    go(core_copy(6))
    for d in (1, 7):
        first_copy(0, d, 0).wait_recv()
        go(core_copy(d))

    @pl.when(lane == 0)
    def _():
        own_feat.wait()

    @pl.when(lane == 1)
    def _():
        first_copy(1, 0, 0).wait_recv()

    go(core_copy(0))
    for d in (2, 6, 1, 7, 0):
        forward(d, 0)
        forward(d, 1)
    own_w.wait()
    for df in range(1, SIDE):
        w_copy(df).wait_recv()
    w_turned[...] = w_all[...].reshape(256, 256).astype(F32).T.astype(BF16)
    for way in range(2):
        second_copy(way, 0).wait_recv()
        second_copy(way, 1).wait_recv()
        go(core_copy(3 if way == 0 else 5))
    for way in range(2):
        second_copy(way, 2).wait_recv()
    go(core_copy(4))
    for d in (3, 5, 4):
        forward(d, 0)
    for d in (3, 5, 4):
        forward(d, 1)

    def agg_copy(dr, df):
        return remote(
            agg_out.at[(f + df) % SIDE], agg_in.at[r, f], agg_send.at[dr, df], agg_recv.at[dr, df], at(dr=dr, df=df)
        )

    group = [(dr, df) for df in (2, 1, 3, 0) for dr in (1, 0) if dr or df]
    for b in range(SIDE):
        agg_out[b] = agg[:, b * TILE:(b + 1) * TILE].astype(BF16)
    for dr, df in group:
        go(agg_copy(dr, df))
    agg_in[r, f] = agg_out[f]
    own_cot.wait()
    for df in range(1, SIDE):
        cot_copy(df).wait_recv()
    for dr, df in group:
        agg_copy(dr, df).wait_recv()
    summed = (agg_in[0].astype(F32) + agg_in[1].astype(F32)).reshape(256, TILE).astype(BF16)
    pre_act = jnp.dot(w_turned[...], summed, preferred_element_type=F32)
    gate = 1.0 / (1.0 + jnp.exp(-pre_act))
    grad = cot_all[...].reshape(256, TILE).astype(F32)
    pre_grad = (grad * gate * (1.0 + pre_act * (1.0 - gate))).astype(BF16)
    signal = jnp.dot(w_all[...].reshape(256, 256), pre_grad, preferred_element_type=F32)
    sig_out[...] = signal.astype(BF16).reshape(SIDE, ROWS, TILE)

    def sig_copy(df):
        return remote(sig_out.at[(f + df) % SIDE], sig_in.at[f], sig_send.at[df], sig_recv.at[df], at(df=df))

    for df in (2, 1, 3):
        go(sig_copy(df))
    sig_in[f] = sig_out[f]

    hid_out[...] = (pre_act * gate).astype(BF16).reshape(SIDE, ROWS, TILE)

    def hid_copy(df):
        return remote(
            hid_out.at[(f + df) % SIDE], hid.at[:, own_lanes], hid_send.at[df], hid_recv.at[df], at(df=df)
        )

    own_hid = pltpu.make_async_copy(hid_out.at[f], hid.at[:, own_lanes], local_sem.at[6])
    own_hid.start()
    for df in range(1, SIDE):
        go(hid_copy(df))
    grad_rows = jnp.where(r == 0, pre_grad[:TILE].astype(F32), pre_grad[TILE:].astype(F32)).astype(BF16)
    share = lax.dot_general(summed, grad_rows, (((1,), (1,)), ((), ())), preferred_element_type=F32)
    g1_out[...] = share.reshape(SIDE, ROWS, TILE)

    def g1_copy(df):
        return remote(g1_out.at[(f + df) % SIDE], g1.at[f], g1_send.at[df], g1_recv.at[df], at(df=df))

    for df in range(1, SIDE):
        go(g1_copy(df))
    g1[f] = g1_out[f]

    for df in (2, 1, 3):
        sig_copy(df).wait_recv()
    signal_row = jnp.concatenate([sig_in[b] for b in range(SIDE)], axis=1)

    def backward(d, cc):
        return jnp.dot(signal_row, dense[PLACE[d, cc]], preferred_element_type=F32)

    def back_copy(d):
        return remote(back_out.at[d], back_in.at[d], back_send.at[d], back_recv.at[d], at(dc=1))

    def give(d):
        back_out[d] = backward(d, 1).astype(BF16)
        go(back_copy(d))

    def take(d):
        keep[d] = backward(d, 0)
        back_copy(d).wait_recv()
        keep[d] += back_in[d].astype(F32)

    def near_copy(way, part):
        d = 4 if part == 2 else (3 if way == 0 else 5)
        step = 2 if part == 2 else 1
        span = pl.ds((part if part < 2 else way) * HALF, HALF)
        return remote(
            near_out.at[way, step - 1, span], near_in.at[way, step - 1, span],
            near_send.at[way, part], near_recv.at[way, part], at(dz=RING - step if way == 0 else step),
        )

    def root_copy(d, chunk, from_lane):
        span = pl.ds(chunk * HALF, HALF) if d in (2, 6) else pl.ds(0, ROWS)
        return remote(
            root_out.at[DIRECT[d], span], root_in.at[from_lane, DIRECT[d], span],
            root_send.at[DIRECT[d], chunk], root_recv.at[from_lane, DIRECT[d], chunk],
            at(dz=RING - d, dx=from_lane, dc=from_lane),
        )

    halves = [slice(0, HALF), slice(HALF, ROWS)]
    for d in (4, 3, 5):
        give(d)
    take(4)
    for way in range(2):
        near_out[way, 1, halves[way]] = keep[4, halves[way]].astype(BF16)
        go(near_copy(way, 2))
    for way in range(2):
        take(3 if way == 0 else 5)
        near_out[way, 0] = keep[3 if way == 0 else 5].astype(BF16)
        go(near_copy(way, way))
        go(near_copy(way, 1 - way))
    for d in (1, 7, 0, 2, 6):
        give(d)

    for df in range(1, SIDE):
        g1_copy(df).wait_recv()
    g2_out[...] = (g1[0] + g1[1]) + (g1[2] + g1[3])

    def g2_copy(dz):
        rows = pl.ds(pl.multiple_of(((z + dz) % RING) * 8, 8), 8)
        return remote(g2_out.at[rows], g2.at[z], g2_send.at[dz], g2_recv.at[dz], at(dz=dz))

    for dz in range(1, RING):
        go(g2_copy(dz))
    g2[z] = g2_out[pl.ds(pl.multiple_of(z * 8, 8), 8)]

    for d in (1, 7):
        take(d)
        root_out[DIRECT[d]] = keep[d].astype(BF16)
        go(root_copy(d, 0, lane))
    take(0)

    @pl.when(lane == 1)
    def _():
        root_out[DIRECT[0]] = keep[0].astype(BF16)
        root_copy(0, 0, lane).start()

    take(2)
    take(6)

    for dz in range(1, RING):
        g2_copy(dz).wait_recv()
    g3_out[...] = jnp.sum(g2[...], axis=0)

    def g3_copy(i):
        return remote(
            g3_out, g3.at[r * 4 + xh * 2 + c], g3_send.at[i], g3_recv.at[i],
            at(dx=i // 4, dc=(i // 2) % 2, dr=i % 2),
        )

    for i in range(1, 8):
        go(g3_copy(i))
    g3[r * 4 + xh * 2 + c] = g3_out[...]

    for i in range(2):
        for way in range(2):
            chunk, d = i ^ way, 2 if way == 0 else 6
            value = keep[d, halves[chunk]]
            near_copy(way, chunk).wait_recv()
            value = value + near_in[way, 0, halves[chunk]].astype(F32)
            if i == 0:
                near_copy(way, 2).wait_recv()
                value = value + near_in[way, 1, halves[chunk]].astype(F32)
            root_out[DIRECT[d], halves[chunk]] = value.astype(BF16)
            go(root_copy(d, chunk, lane))

    for i in range(1, 8):
        g3_copy(i).wait_recv()
    scale = float(NODES * PARTS) ** -0.5
    for half in range(2):
        four = (g3[4 * half] + g3[4 * half + 1]) + (g3[4 * half + 2] + g3[4 * half + 3])
        g4_out[:, half * TILE:(half + 1) * TILE] = four * scale
    own_rows = pl.ds(pl.multiple_of(z * 8, 8), 8)

    def g4_copy(dz):
        return remote(g4_out, wgrad.at[own_rows], g4_send.at[dz], g4_recv.at[dz], at(dz=dz))

    for dz in range(1, RING):
        go(g4_copy(dz))
    own_wgrad = pltpu.make_async_copy(g4_out, wgrad.at[own_rows], local_sem.at[7])
    own_wgrad.start()

    def fin_copy(chunk):
        span = pl.ds(chunk * HALF, HALF)
        return remote(done.at[span], igrad.at[span], fin_send.at[chunk], fin_recv.at[chunk], at(dr=1))

    own_igrad = pltpu.make_async_copy(done, igrad, local_sem.at[8])

    @pl.when(lane == 0)
    def _():
        for from_lane in range(2):
            for d in (1, 7, 0) if from_lane else (1, 7):
                root_copy(d, 0, from_lane).wait_recv()
        for chunk in range(2):
            value = keep[0, halves[chunk]]
            for from_lane in range(2):
                for d in (1, 7, 0) if from_lane else (1, 7):
                    value = value + root_in[from_lane, DIRECT[d], halves[chunk]].astype(F32)
            for from_lane in range(2):
                for d in (2, 6):
                    root_copy(d, chunk, from_lane).wait_recv()
                    value = value + root_in[from_lane, DIRECT[d], halves[chunk]].astype(F32)
            done[halves[chunk]] = value.astype(BF16)
            fin_copy(chunk).start()
        own_igrad.start()

    @pl.when(lane == 1)
    def _():
        for chunk in range(2):
            fin_copy(chunk).wait_recv()

    @pl.when(lane == 0)
    def _():
        for first in firsts:
            first_copy(*first).wait_send()
        for chunk in range(2):
            fin_copy(chunk).wait_send()
        own_igrad.wait()

    @pl.when(lane == 1)
    def _():
        root_copy(0, 0, lane).wait_send()

    for copy in pending:
        copy.wait_send()
    for df in range(1, SIDE):
        hid_copy(df).wait_recv()
    for dz in range(1, RING):
        g4_copy(dz).wait_recv()
    own_hid.wait()
    own_wgrad.wait()


def hand_over(hid, wgrad, igrad, hid_to, wgrad_to, igrad_to, sems):
    copies = [
        pltpu.make_async_copy(src, dst, sems.at[i])
        for i, (src, dst) in enumerate(((hid, hid_to), (wgrad, wgrad_to), (igrad, igrad_to)))
    ]
    for copy in copies:
        copy.start()
    for copy in copies:
        copy.wait()


def body(features_t, tile_values, tile_rows, tile_cols, tile_count, weight, cotangent_t):
    anywhere = pl.BlockSpec(memory_space=pl.ANY)
    vmem, dma = pltpu.VMEM, pltpu.SemaphoreType.DMA
    block = (SIDE, ROWS, TILE)
    panel = (ROWS, NODES)
    out_shape = (
        jax.ShapeDtypeStruct((ROWS, NODES), BF16),
        jax.ShapeDtypeStruct((ROWS, 256), F32),
        jax.ShapeDtypeStruct((ROWS, NODES), BF16),
    )
    results = pl.pallas_call(
        kernel,
        out_shape=out_shape,
        in_specs=[anywhere] * 7,
        out_specs=(anywhere, anywhere, anywhere),
        scratch_shapes=[
            pltpu.SMEM((SLOTS, 1, PARTS), jnp.int32),
            pltpu.SMEM((SLOTS, 1, PARTS), jnp.int32),
            pltpu.SMEM((1, PARTS), jnp.int32),
            vmem((16, SLOTS, TILE, TILE), BF16),
            vmem((SLOTS + 1, TILE, TILE), BF16),
            vmem((16, NODES, NODES), BF16),
            vmem((RING, 2, *panel), BF16),
            vmem(panel, F32),
            vmem((SIDE, ROWS, 256), BF16),
            vmem((256, 256), BF16),
            vmem(block, BF16),
            vmem(block, BF16),
            vmem((2, *block), BF16),
            vmem(block, BF16),
            vmem(block, BF16),
            vmem(block, BF16),
            vmem(block, F32),
            vmem(block, F32),
            vmem((ROWS, TILE), F32),
            vmem((RING, 8, TILE), F32),
            vmem((8, TILE), F32),
            vmem((8, 8, TILE), F32),
            vmem((8, 256), F32),
            vmem((RING, *panel), BF16),
            vmem((RING, *panel), BF16),
            vmem((RING, *panel), F32),
            vmem((2, 2, *panel), BF16),
            vmem((2, 2, *panel), BF16),
            vmem((5, *panel), BF16),
            vmem((2, 5, *panel), BF16),
            vmem(panel, BF16),
            dma((16,)), dma((9,)), dma((2, 5, 2)), dma((5, 2)), dma((2, 3)), dma((2, 3)), dma((RING,)), dma((RING,)),
            dma((SIDE,)), dma((SIDE,)), dma((SIDE,)), dma((SIDE,)),
            dma((2, SIDE)), dma((2, SIDE)), dma((SIDE,)), dma((SIDE,)),
            dma((SIDE,)), dma((SIDE,)), dma((SIDE,)), dma((SIDE,)),
            dma((RING,)), dma((RING,)), dma((8,)), dma((8,)), dma((RING,)), dma((RING,)),
            dma((RING,)), dma((RING,)), dma((2, 3)), dma((2, 3)), dma((5, 2)), dma((2, 5, 2)), dma((2,)), dma((2,)),
        ],
        compiler_params=pltpu.CompilerParams(
            collective_id=0, has_side_effects=True, vmem_limit_bytes=VMEM_BYTES
        ),
    )(
        features_t, tile_values, jnp.transpose(tile_rows, (2, 0, 1)), jnp.transpose(tile_cols, (2, 0, 1)),
        tile_count, weight, cotangent_t,
    )
    return pl.pallas_call(
        hand_over,
        out_shape=out_shape,
        in_specs=[anywhere] * 3,
        out_specs=(anywhere,) * 3,
        scratch_shapes=[dma((3,))],
    )(*results)


def solution(mesh):
    return jax.shard_map(
        body,
        mesh=mesh,
        in_specs=(
            P("feat", "blk"),
            P("blk", None, None, None, None),
            P("blk", None, None),
            P("blk", None, None),
            P("blk", None),
            P("feat", None),
            P("feat", "blk"),
        ),
        out_specs=(P("feat", "blk"), P("feat", None), P("feat", "blk")),
        check_vma=False,
    )
```

time: 74.8 us -> 58.9 us (0.79)
  local copies, waits for them, and re-layouts: 11.1 us -> 0 us
  Pallas kernels: 62.7 us -> 58.2 us
    unnamed x15 -> x0, local copies, waits for them, and re-layouts: 11.1 us -> none
    pallas_call x1 -> x2, Pallas kernels: 62.7 us -> 58.2 us  [the longest x1 51.1 us: body(): pl.pallas_call(kernel, out_shape=out_shape, in_specs=[anywhere] * 7, out_...]
where the time goes in v2:
time: 58.9 us
  Pallas kernels  58.2 us (99%)
  between operations  0.64 us (1%)
    pallas_call x1, Pallas kernels, body(): pl.pallas_call(kernel, out_shape=out_shape, in_specs=[anywhere] * 7, out_...  51.1 us
    pallas_call x1, Pallas kernels, body(): pl.pallas_call(hand_over, out_shape=out_shape, in_specs=[anywhere] * 3, o...  7.09 us

profile of v2, /device:TPU:1, one launch (start us, length us, event | category | flops | bytes accessed | tf_op | source)
XLA Modules:
  0.0 58.9 jit_solution(12362051490963134891)
XLA Ops:
  0.6 51.1 %shard_map.94 = (bf16[64,512]{1,0:T(8,128)(2,1)}, f32[64,256]{1,0:T(8,128)}, bf16[64,512]{1,0:T(8,128)(2,1)}) custom-call(bf16[64,512]{1,0:T(8,128)(2,1)} %feat.1, bf16[1,32,12,128,128]{4,3,2,1,0:T(8,128)(2,1)} %tiles.1, s32[12,1,32]{2,1,0:T(1,128)} %bitcast.2, s32[12,1,32]{2,1,0:T(1,128)} %bitcast.3, s32[1,32]{1,0:T(1,128)} %count_hbm.1, ...), custom_call_target="tpu_custom_call" | custom-call | tf_op jit(solution)/shard_map/pallas_call | solution.py:459
  51.8 7.1 %shard_map.95 = (bf16[64,512]{1,0:T(8,128)(2,1)}, f32[64,256]{1,0:T(8,128)}, bf16[64,512]{1,0:T(8,128)(2,1)}) custom-call(bf16[64,512]{1,0:T(8,128)(2,1)} %get-tuple-element.6.hid, f32[64,256]{1,0:T(8,128)} %get-tuple-element.7.wgrad, bf16[64,512]{1,0:T(8,128)(2,1)} %get-tuple-element.8.igrad), custom_call_target="tpu_custom_call" | custom-call | tf_op jit(solution)/shard_map/pallas_call | solution.py:510

commit v3 on v2

--- a/solution.py
+++ b/solution.py
@@ -55,6 +55,14 @@
             src_ref=src, dst_ref=dst, send_sem=send, recv_sem=recv, device_id=device, device_id_type=MESH
         )
 
+    partners = [at(dz=dz) for dz in (4, 3, 5, 2, 6, 1, 7)]
+    partners += [at(dz=dz, dx=1, dc=1) for dz in (2, 6, 1, 7, 0)]
+    partners += [at(dr=dr, df=df) for df in (2, 1, 3, 0) for dr in range(2) if dr or df]
+    partners += [at(dc=1), at(dx=1), at(dx=1, dr=1), at(dc=1, dr=1), at(dx=1, dc=1, dr=1)]
+    barrier = pltpu.get_barrier_semaphore()
+    for device in partners:
+        pl.semaphore_signal(barrier, inc=1, device_id=device, device_id_type=MESH)
+
     def tile_copy(n):
         half = n // 2
         odd, step = half % 2, (half + 1) // 2
@@ -88,13 +96,6 @@
 
     lax.fori_loop(0, 16, start_tiles, 0)
 
-    partners = [at(dz=dz) for dz in (4, 3, 5, 2, 6, 1, 7)]
-    partners += [at(dz=dz, dx=1, dc=1) for dz in (2, 6, 1, 7, 0)]
-    partners += [at(dr=dr, df=df) for df in (2, 1, 3, 0) for dr in range(2) if dr or df]
-    partners += [at(dc=1), at(dx=1), at(dx=1, dr=1), at(dc=1, dr=1), at(dx=1, dc=1, dr=1)]
-    barrier = pltpu.get_barrier_semaphore()
-    for device in partners:
-        pl.semaphore_signal(barrier, inc=1, device_id=device, device_id_type=MESH)
     acc[SLOTS] = jnp.zeros((TILE, TILE), BF16)
     agg[...] = jnp.zeros_like(agg)
     pl.semaphore_wait(barrier, len(partners))
@@ -243,6 +244,17 @@
         go(sig_copy(df))
     sig_in[f] = sig_out[f]
 
+    grad_rows = jnp.where(r == 0, pre_grad[:TILE].astype(F32), pre_grad[TILE:].astype(F32)).astype(BF16)
+    share = lax.dot_general(summed, grad_rows, (((1,), (1,)), ((), ())), preferred_element_type=F32)
+    g1_out[...] = share.astype(BF16).reshape(SIDE, ROWS, TILE)
+
+    def g1_copy(df):
+        return remote(g1_out.at[(f + df) % SIDE], g1.at[f], g1_send.at[df], g1_recv.at[df], at(df=df))
+
+    for df in range(1, SIDE):
+        go(g1_copy(df))
+    g1[f] = g1_out[f]
+
     hid_out[...] = (pre_act * gate).astype(BF16).reshape(SIDE, ROWS, TILE)
 
     def hid_copy(df):
@@ -254,16 +266,6 @@
     own_hid.start()
     for df in range(1, SIDE):
         go(hid_copy(df))
-    grad_rows = jnp.where(r == 0, pre_grad[:TILE].astype(F32), pre_grad[TILE:].astype(F32)).astype(BF16)
-    share = lax.dot_general(summed, grad_rows, (((1,), (1,)), ((), ())), preferred_element_type=F32)
-    g1_out[...] = share.reshape(SIDE, ROWS, TILE)
-
-    def g1_copy(df):
-        return remote(g1_out.at[(f + df) % SIDE], g1.at[f], g1_send.at[df], g1_recv.at[df], at(df=df))
-
-    for df in range(1, SIDE):
-        go(g1_copy(df))
-    g1[f] = g1_out[f]
 
     for df in (2, 1, 3):
         sig_copy(df).wait_recv()
@@ -318,7 +320,7 @@
 
     for df in range(1, SIDE):
         g1_copy(df).wait_recv()
-    g2_out[...] = (g1[0] + g1[1]) + (g1[2] + g1[3])
+    g2_out[...] = jnp.sum(g1[...].astype(F32), axis=0)
 
     def g2_copy(dz):
         rows = pl.ds(pl.multiple_of(((z + dz) % RING) * 8, 8), 8)
@@ -341,20 +343,6 @@
 
     take(2)
     take(6)
-
-    for dz in range(1, RING):
-        g2_copy(dz).wait_recv()
-    g3_out[...] = jnp.sum(g2[...], axis=0)
-
-    def g3_copy(i):
-        return remote(
-            g3_out, g3.at[r * 4 + xh * 2 + c], g3_send.at[i], g3_recv.at[i],
-            at(dx=i // 4, dc=(i // 2) % 2, dr=i % 2),
-        )
-
-    for i in range(1, 8):
-        go(g3_copy(i))
-    g3[r * 4 + xh * 2 + c] = g3_out[...]
 
     for i in range(2):
         for way in range(2):
@@ -368,21 +356,19 @@
             root_out[DIRECT[d], halves[chunk]] = value.astype(BF16)
             go(root_copy(d, chunk, lane))
 
+    for dz in range(1, RING):
+        g2_copy(dz).wait_recv()
+    g3_out[...] = jnp.sum(g2[...], axis=0)
+
+    def g3_copy(i):
+        return remote(
+            g3_out, g3.at[r * 4 + xh * 2 + c], g3_send.at[i], g3_recv.at[i],
+            at(dx=i // 4, dc=(i // 2) % 2, dr=i % 2),
+        )
+
     for i in range(1, 8):
-        g3_copy(i).wait_recv()
-    scale = float(NODES * PARTS) ** -0.5
-    for half in range(2):
-        four = (g3[4 * half] + g3[4 * half + 1]) + (g3[4 * half + 2] + g3[4 * half + 3])
-        g4_out[:, half * TILE:(half + 1) * TILE] = four * scale
-    own_rows = pl.ds(pl.multiple_of(z * 8, 8), 8)
-
-    def g4_copy(dz):
-        return remote(g4_out, wgrad.at[own_rows], g4_send.at[dz], g4_recv.at[dz], at(dz=dz))
-
-    for dz in range(1, RING):
-        go(g4_copy(dz))
-    own_wgrad = pltpu.make_async_copy(g4_out, wgrad.at[own_rows], local_sem.at[7])
-    own_wgrad.start()
+        go(g3_copy(i))
+    g3[r * 4 + xh * 2 + c] = g3_out[...]
 
     def fin_copy(chunk):
         span = pl.ds(chunk * HALF, HALF)
@@ -408,6 +394,22 @@
             fin_copy(chunk).start()
         own_igrad.start()
 
+    for i in range(1, 8):
+        g3_copy(i).wait_recv()
+    scale = float(NODES * PARTS) ** -0.5
+    for half in range(2):
+        four = (g3[4 * half] + g3[4 * half + 1]) + (g3[4 * half + 2] + g3[4 * half + 3])
+        g4_out[:, half * TILE:(half + 1) * TILE] = four * scale
+    own_rows = pl.ds(pl.multiple_of(z * 8, 8), 8)
+
+    def g4_copy(dz):
+        return remote(g4_out, wgrad.at[own_rows], g4_send.at[dz], g4_recv.at[dz], at(dz=dz))
+
+    for dz in range(1, RING):
+        go(g4_copy(dz))
+    own_wgrad = pltpu.make_async_copy(g4_out, wgrad.at[own_rows], local_sem.at[7])
+    own_wgrad.start()
+
     @pl.when(lane == 1)
     def _():
         for chunk in range(2):
@@ -435,15 +437,10 @@
     own_wgrad.wait()
 
 
-def hand_over(hid, wgrad, igrad, hid_to, wgrad_to, igrad_to, sems):
-    copies = [
-        pltpu.make_async_copy(src, dst, sems.at[i])
-        for i, (src, dst) in enumerate(((hid, hid_to), (wgrad, wgrad_to), (igrad, igrad_to)))
-    ]
-    for copy in copies:
-        copy.start()
-    for copy in copies:
-        copy.wait()
+def hand_over(hid, wgrad, igrad, hid_to, wgrad_to, igrad_to):
+    hid_to[...] = hid[...]
+    wgrad_to[...] = wgrad[...]
+    igrad_to[...] = igrad[...]
 
 
 def body(features_t, tile_values, tile_rows, tile_cols, tile_count, weight, cotangent_t):
@@ -478,8 +475,8 @@
             vmem(block, BF16),
             vmem(block, BF16),
             vmem(block, BF16),
-            vmem(block, F32),
-            vmem(block, F32),
+            vmem(block, BF16),
+            vmem(block, BF16),
             vmem((ROWS, TILE), F32),
             vmem((RING, 8, TILE), F32),
             vmem((8, TILE), F32),
@@ -510,9 +507,8 @@
     return pl.pallas_call(
         hand_over,
         out_shape=out_shape,
-        in_specs=[anywhere] * 3,
-        out_specs=(anywhere,) * 3,
-        scratch_shapes=[dma((3,))],
+        in_specs=[pl.BlockSpec(memory_space=vmem)] * 3,
+        out_specs=(pl.BlockSpec(memory_space=vmem),) * 3,
     )(*results)
 
 

time: 58.9 us -> 52.1 us (0.88)
  Pallas kernels: 58.2 us -> 51.4 us
    pallas_call x1, Pallas kernels: 7.09 us -> 1.58 us  [body(): pl.pallas_call(hand_over, out_shape=out_shape, in_specs=[pl.BlockSpec(mem...]
    pallas_call x1, Pallas kernels: 51.1 us -> 49.8 us  [body(): pl.pallas_call(kernel, out_shape=out_shape, in_specs=[anywhere] * 7, out_...]
where the time goes in v3:
time: 52.1 us; the launch traced here: 52 us
  Pallas kernels  51.4 us (99%)
  between operations  0.64 us (1%)
    pallas_call x1, Pallas kernels, body(): pl.pallas_call(kernel, out_shape=out_shape, in_specs=[anywhere] * 7, out_...  49.8 us
    pallas_call x1, Pallas kernels, body(): pl.pallas_call(hand_over, out_shape=out_shape, in_specs=[pl.BlockSpec(mem...  1.58 us

profile of v3, /device:TPU:1, one launch (start us, length us, event | category | flops | bytes accessed | tf_op | source)
XLA Modules:
  0.0 52.0 jit_solution(5384161375665269651)
XLA Ops:
  0.6 49.8 %shard_map.94 = (bf16[64,512]{1,0:T(8,128)(2,1)}, f32[64,256]{1,0:T(8,128)}, bf16[64,512]{1,0:T(8,128)(2,1)}) custom-call(bf16[64,512]{1,0:T(8,128)(2,1)} %feat.1, bf16[1,32,12,128,128]{4,3,2,1,0:T(8,128)(2,1)} %tiles.1, s32[12,1,32]{2,1,0:T(1,128)} %bitcast.2, s32[12,1,32]{2,1,0:T(1,128)} %bitcast.3, s32[1,32]{1,0:T(1,128)} %count_hbm.1, ...), custom_call_target="tpu_custom_call" | custom-call | tf_op jit(solution)/shard_map/pallas_call | solution.py:456
  50.4 1.6 %shard_map.95 = (bf16[64,512]{1,0:T(8,128)(2,1)}, f32[64,256]{1,0:T(8,128)}, bf16[64,512]{1,0:T(8,128)(2,1)}) custom-call(bf16[64,512]{1,0:T(8,128)(2,1)} %get-tuple-element.6.hid, f32[64,256]{1,0:T(8,128)} %get-tuple-element.7.wgrad, bf16[64,512]{1,0:T(8,128)(2,1)} %get-tuple-element.8.igrad), custom_call_target="tpu_custom_call" | custom-call | tf_op jit(solution)/shard_map/pallas_call | solution.py:507

commit v4 on v3

--- a/solution.py
+++ b/solution.py
@@ -29,7 +29,7 @@
     raw, acc, dense, panels, agg, w_all, w_turned, cot_all,
     agg_out, agg_in, hid_out, sig_out, sig_in,
     g1_out, g1, g2_out, g2, g3_out, g3, g4_out,
-    back_out, back_in, keep, near_out, near_in, root_out, root_in, done,
+    back_out, back_in, keep, near_out, near_in, root_out, root_in, fin_out, fin_in, done,
     tile_sem, local_sem, first_send, first_recv, second_send, second_recv, core_send, core_recv,
     w_send, w_recv, cot_send, cot_recv, agg_send, agg_recv, sig_send, sig_recv,
     hid_send, hid_recv, g1_send, g1_recv, g2_send, g2_recv, g3_send, g3_recv, g4_send, g4_recv,
@@ -56,9 +56,9 @@
         )
 
     partners = [at(dz=dz) for dz in (4, 3, 5, 2, 6, 1, 7)]
-    partners += [at(dz=dz, dx=1, dc=1) for dz in (2, 6, 1, 7, 0)]
+    partners += [at(dz=dz, dx=1, dc=1, dr=1) for dz in (2, 6, 1, 7, 0)]
     partners += [at(dr=dr, df=df) for df in (2, 1, 3, 0) for dr in range(2) if dr or df]
-    partners += [at(dc=1), at(dx=1), at(dx=1, dr=1), at(dc=1, dr=1), at(dx=1, dc=1, dr=1)]
+    partners += [at(dc=1), at(dx=1), at(dx=1, dr=1), at(dc=1, dr=1), at(dx=1, dc=1)]
     barrier = pltpu.get_barrier_semaphore()
     for device in partners:
         pl.semaphore_signal(barrier, inc=1, device_id=device, device_id_type=MESH)
@@ -100,21 +100,25 @@
     agg[...] = jnp.zeros_like(agg)
     pl.semaphore_wait(barrier, len(partners))
 
-    def first_copy(to_lane, d, chunk):
+    def home(dz):
+        return at(dz=dz, dx=lane, dc=lane, dr=lane)
+
+    def first_copy(d, chunk):
         span = pl.ds(chunk * HALF, HALF) if d in (2, 6) else pl.ds(0, ROWS)
         return remote(
             feat.at[span], panels.at[d, 0, span],
-            first_send.at[to_lane, DIRECT[d], chunk], first_recv.at[DIRECT[d], chunk],
-            at(dz=d, dx=to_lane, dc=to_lane),
-        )
-
-    firsts = [(to_lane, d, i ^ (d == 6)) for i in range(2) for d in (2, 6) for to_lane in (1, 0)]
-    firsts += [(to_lane, d, 0) for d in (1, 7) for to_lane in (1, 0)] + [(1, 0, 0)]
-
-    @pl.when(lane == 0)
-    def _():
-        for first in firsts:
-            first_copy(*first).start()
+            first_send.at[DIRECT[d], chunk], first_recv.at[DIRECT[d], chunk], home(d),
+        )
+
+    for i in range(2):
+        for d in (2, 6):
+            go(first_copy(d, i ^ (d == 6)))
+    for d in (1, 7):
+        go(first_copy(d, 0))
+
+    @pl.when(lane == 1)
+    def _():
+        first_copy(0, 0).start()
 
     def second_copy(way, part):
         d = 2 if way == 0 else RING - 2
@@ -175,14 +179,14 @@
     for i in range(2):
         for way in range(2):
             chunk = i ^ way
-            first_copy(0, 2 if way == 0 else 6, chunk).wait_recv()
+            first_copy(2 if way == 0 else 6, chunk).wait_recv()
             if i == 0:
                 go(second_copy(way, 2))
             go(second_copy(way, chunk))
     go(core_copy(2))
     go(core_copy(6))
     for d in (1, 7):
-        first_copy(0, d, 0).wait_recv()
+        first_copy(d, 0).wait_recv()
         go(core_copy(d))
 
     @pl.when(lane == 0)
@@ -191,7 +195,7 @@
 
     @pl.when(lane == 1)
     def _():
-        first_copy(1, 0, 0).wait_recv()
+        first_copy(0, 0).wait_recv()
 
     go(core_copy(0))
     for d in (2, 6, 1, 7, 0):
@@ -295,12 +299,11 @@
             near_send.at[way, part], near_recv.at[way, part], at(dz=RING - step if way == 0 else step),
         )
 
-    def root_copy(d, chunk, from_lane):
+    def root_copy(d, chunk):
         span = pl.ds(chunk * HALF, HALF) if d in (2, 6) else pl.ds(0, ROWS)
         return remote(
-            root_out.at[DIRECT[d], span], root_in.at[from_lane, DIRECT[d], span],
-            root_send.at[DIRECT[d], chunk], root_recv.at[from_lane, DIRECT[d], chunk],
-            at(dz=RING - d, dx=from_lane, dc=from_lane),
+            root_out.at[DIRECT[d], span], root_in.at[DIRECT[d], span],
+            root_send.at[DIRECT[d], chunk], root_recv.at[DIRECT[d], chunk], home(RING - d),
         )
 
     halves = [slice(0, HALF), slice(HALF, ROWS)]
@@ -310,6 +313,18 @@
     for way in range(2):
         near_out[way, 1, halves[way]] = keep[4, halves[way]].astype(BF16)
         go(near_copy(way, 2))
+    for df in range(1, SIDE):
+        g1_copy(df).wait_recv()
+    g2_out[...] = jnp.sum(g1[...].astype(F32), axis=0)
+
+    def g2_copy(dz):
+        rows = pl.ds(pl.multiple_of(((z + dz) % RING) * 8, 8), 8)
+        return remote(g2_out.at[rows], g2.at[z], g2_send.at[dz], g2_recv.at[dz], at(dz=dz))
+
+    for dz in range(1, RING):
+        go(g2_copy(dz))
+    g2[z] = g2_out[pl.ds(pl.multiple_of(z * 8, 8), 8)]
+
     for way in range(2):
         take(3 if way == 0 else 5)
         near_out[way, 0] = keep[3 if way == 0 else 5].astype(BF16)
@@ -318,31 +333,33 @@
     for d in (1, 7, 0, 2, 6):
         give(d)
 
-    for df in range(1, SIDE):
-        g1_copy(df).wait_recv()
-    g2_out[...] = jnp.sum(g1[...].astype(F32), axis=0)
-
-    def g2_copy(dz):
-        rows = pl.ds(pl.multiple_of(((z + dz) % RING) * 8, 8), 8)
-        return remote(g2_out.at[rows], g2.at[z], g2_send.at[dz], g2_recv.at[dz], at(dz=dz))
-
-    for dz in range(1, RING):
-        go(g2_copy(dz))
-    g2[z] = g2_out[pl.ds(pl.multiple_of(z * 8, 8), 8)]
-
     for d in (1, 7):
         take(d)
         root_out[DIRECT[d]] = keep[d].astype(BF16)
-        go(root_copy(d, 0, lane))
+        go(root_copy(d, 0))
     take(0)
 
     @pl.when(lane == 1)
     def _():
         root_out[DIRECT[0]] = keep[0].astype(BF16)
-        root_copy(0, 0, lane).start()
+        root_copy(0, 0).start()
 
     take(2)
     take(6)
+
+    for dz in range(1, RING):
+        g2_copy(dz).wait_recv()
+    g3_out[...] = jnp.sum(g2[...], axis=0)
+
+    def g3_copy(i):
+        return remote(
+            g3_out, g3.at[r * 4 + xh * 2 + c], g3_send.at[i], g3_recv.at[i],
+            at(dx=i // 4, dc=(i // 2) % 2, dr=i % 2),
+        )
+
+    for i in range(1, 8):
+        go(g3_copy(i))
+    g3[r * 4 + xh * 2 + c] = g3_out[...]
 
     for i in range(2):
         for way in range(2):
@@ -354,45 +371,7 @@
                 near_copy(way, 2).wait_recv()
                 value = value + near_in[way, 1, halves[chunk]].astype(F32)
             root_out[DIRECT[d], halves[chunk]] = value.astype(BF16)
-            go(root_copy(d, chunk, lane))
-
-    for dz in range(1, RING):
-        g2_copy(dz).wait_recv()
-    g3_out[...] = jnp.sum(g2[...], axis=0)
-
-    def g3_copy(i):
-        return remote(
-            g3_out, g3.at[r * 4 + xh * 2 + c], g3_send.at[i], g3_recv.at[i],
-            at(dx=i // 4, dc=(i // 2) % 2, dr=i % 2),
-        )
-
-    for i in range(1, 8):
-        go(g3_copy(i))
-    g3[r * 4 + xh * 2 + c] = g3_out[...]
-
-    def fin_copy(chunk):
-        span = pl.ds(chunk * HALF, HALF)
-        return remote(done.at[span], igrad.at[span], fin_send.at[chunk], fin_recv.at[chunk], at(dr=1))
-
-    own_igrad = pltpu.make_async_copy(done, igrad, local_sem.at[8])
-
-    @pl.when(lane == 0)
-    def _():
-        for from_lane in range(2):
-            for d in (1, 7, 0) if from_lane else (1, 7):
-                root_copy(d, 0, from_lane).wait_recv()
-        for chunk in range(2):
-            value = keep[0, halves[chunk]]
-            for from_lane in range(2):
-                for d in (1, 7, 0) if from_lane else (1, 7):
-                    value = value + root_in[from_lane, DIRECT[d], halves[chunk]].astype(F32)
-            for from_lane in range(2):
-                for d in (2, 6):
-                    root_copy(d, chunk, from_lane).wait_recv()
-                    value = value + root_in[from_lane, DIRECT[d], halves[chunk]].astype(F32)
-            done[halves[chunk]] = value.astype(BF16)
-            fin_copy(chunk).start()
-        own_igrad.start()
+            go(root_copy(d, chunk))
 
     for i in range(1, 8):
         g3_copy(i).wait_recv()
@@ -410,22 +389,39 @@
     own_wgrad = pltpu.make_async_copy(g4_out, wgrad.at[own_rows], local_sem.at[7])
     own_wgrad.start()
 
+    def fin_copy(chunk):
+        span = pl.ds(chunk * HALF, HALF)
+        return remote(fin_out.at[span], fin_in.at[span], fin_send.at[chunk], fin_recv.at[chunk], at(dr=1))
+
+    @pl.when(lane == 0)
+    def _():
+        root_in[DIRECT[0]] = keep[0].astype(BF16)
+
     @pl.when(lane == 1)
     def _():
-        for chunk in range(2):
-            fin_copy(chunk).wait_recv()
-
-    @pl.when(lane == 0)
-    def _():
-        for first in firsts:
-            first_copy(*first).wait_send()
-        for chunk in range(2):
-            fin_copy(chunk).wait_send()
-        own_igrad.wait()
+        root_copy(0, 0).wait_recv()
+
+    for d in (1, 7):
+        root_copy(d, 0).wait_recv()
+    for chunk in range(2):
+        value = root_in[DIRECT[0], halves[chunk]].astype(F32)
+        for d in (1, 7, 2, 6):
+            if d in (2, 6):
+                root_copy(d, chunk).wait_recv()
+            value = value + root_in[DIRECT[d], halves[chunk]].astype(F32)
+        fin_out[halves[chunk]] = value.astype(BF16)
+        go(fin_copy(chunk))
+
+    for chunk in range(2):
+        fin_copy(chunk).wait_recv()
+    done[...] = (fin_out[...].astype(F32) + fin_in[...].astype(F32)).astype(BF16)
+    own_igrad = pltpu.make_async_copy(done, igrad, local_sem.at[8])
+    own_igrad.start()
 
     @pl.when(lane == 1)
     def _():
-        root_copy(0, 0, lane).wait_send()
+        first_copy(0, 0).wait_send()
+        root_copy(0, 0).wait_send()
 
     for copy in pending:
         copy.wait_send()
@@ -435,6 +431,7 @@
         g4_copy(dz).wait_recv()
     own_hid.wait()
     own_wgrad.wait()
+    own_igrad.wait()
 
 
 def hand_over(hid, wgrad, igrad, hid_to, wgrad_to, igrad_to):
@@ -488,14 +485,16 @@
             vmem((2, 2, *panel), BF16),
             vmem((2, 2, *panel), BF16),
             vmem((5, *panel), BF16),
-            vmem((2, 5, *panel), BF16),
+            vmem((5, *panel), BF16),
             vmem(panel, BF16),
-            dma((16,)), dma((9,)), dma((2, 5, 2)), dma((5, 2)), dma((2, 3)), dma((2, 3)), dma((RING,)), dma((RING,)),
+            vmem(panel, BF16),
+            vmem(panel, BF16),
+            dma((16,)), dma((9,)), dma((5, 2)), dma((5, 2)), dma((2, 3)), dma((2, 3)), dma((RING,)), dma((RING,)),
             dma((SIDE,)), dma((SIDE,)), dma((SIDE,)), dma((SIDE,)),
             dma((2, SIDE)), dma((2, SIDE)), dma((SIDE,)), dma((SIDE,)),
             dma((SIDE,)), dma((SIDE,)), dma((SIDE,)), dma((SIDE,)),
             dma((RING,)), dma((RING,)), dma((8,)), dma((8,)), dma((RING,)), dma((RING,)),
-            dma((RING,)), dma((RING,)), dma((2, 3)), dma((2, 3)), dma((5, 2)), dma((2, 5, 2)), dma((2,)), dma((2,)),
+            dma((RING,)), dma((RING,)), dma((2, 3)), dma((2, 3)), dma((5, 2)), dma((5, 2)), dma((2,)), dma((2,)),
         ],
         compiler_params=pltpu.CompilerParams(
             collective_id=0, has_side_effects=True, vmem_limit_bytes=VMEM_BYTES

time: 52.1 us -> 50.3 us (0.965)
  Pallas kernels: 51.4 us -> 49.5 us
    pallas_call x1, Pallas kernels: 49.8 us -> 47.9 us  [body(): pl.pallas_call(kernel, out_shape=out_shape, in_specs=[anywhere] * 7, out_...]
where the time goes in v4:
time: 50.3 us; the launch traced here: 50.2 us
  Pallas kernels  49.5 us (98%)
  between operations  0.64 us (1%)
    pallas_call x1, Pallas kernels, body(): pl.pallas_call(kernel, out_shape=out_shape, in_specs=[anywhere] * 7, out_...  47.9 us
    pallas_call x1, Pallas kernels, body(): pl.pallas_call(hand_over, out_shape=out_shape, in_specs=[pl.BlockSpec(mem...  1.58 us

profile of v4, /device:TPU:1, one launch (start us, length us, event | category | flops | bytes accessed | tf_op | source)
XLA Modules:
  0.0 50.2 jit_solution(2369918588588426912)
XLA Ops:
  0.6 47.9 %shard_map.94 = (bf16[64,512]{1,0:T(8,128)(2,1)}, f32[64,256]{1,0:T(8,128)}, bf16[64,512]{1,0:T(8,128)(2,1)}) custom-call(bf16[64,512]{1,0:T(8,128)(2,1)} %feat.1, bf16[1,32,12,128,128]{4,3,2,1,0:T(8,128)(2,1)} %tiles.1, s32[12,1,32]{2,1,0:T(1,128)} %bitcast.2, s32[12,1,32]{2,1,0:T(1,128)} %bitcast.3, s32[1,32]{1,0:T(1,128)} %count_hbm.1, ...), custom_call_target="tpu_custom_call" | custom-call | tf_op jit(solution)/shard_map/pallas_call | solution.py:453
  48.6 1.6 %shard_map.95 = (bf16[64,512]{1,0:T(8,128)(2,1)}, f32[64,256]{1,0:T(8,128)}, bf16[64,512]{1,0:T(8,128)(2,1)}) custom-call(bf16[64,512]{1,0:T(8,128)(2,1)} %get-tuple-element.6.hid, f32[64,256]{1,0:T(8,128)} %get-tuple-element.7.wgrad, bf16[64,512]{1,0:T(8,128)(2,1)} %get-tuple-element.8.igrad), custom_call_target="tpu_custom_call" | custom-call | tf_op jit(solution)/shard_map/pallas_call | solution.py:506

commit v5 on v4

--- a/solution.py
+++ b/solution.py
@@ -24,12 +24,12 @@
 
 def kernel(
     feat, tiles, rows_hbm, cols_hbm, count_hbm, weight, cot,
-    hid, wgrad, igrad,
+    hid, wgrad, fin_own, fin_other,
     tile_rows, tile_cols, tile_count,
     raw, acc, dense, panels, agg, w_all, w_turned, cot_all,
     agg_out, agg_in, hid_out, sig_out, sig_in,
     g1_out, g1, g2_out, g2, g3_out, g3, g4_out,
-    back_out, back_in, keep, near_out, near_in, root_out, root_in, fin_out, fin_in, done,
+    back_out, back_in, keep, near_out, near_in, root_out, root_in, fin_out,
     tile_sem, local_sem, first_send, first_recv, second_send, second_recv, core_send, core_recv,
     w_send, w_recv, cot_send, cot_recv, agg_send, agg_recv, sig_send, sig_recv,
     hid_send, hid_recv, g1_send, g1_recv, g2_send, g2_recv, g3_send, g3_recv, g4_send, g4_recv,
@@ -209,11 +209,12 @@
         second_copy(way, 0).wait_recv()
         second_copy(way, 1).wait_recv()
         go(core_copy(3 if way == 0 else 5))
+    forward(3, 0)
     for way in range(2):
         second_copy(way, 2).wait_recv()
     go(core_copy(4))
-    for d in (3, 5, 4):
-        forward(d, 0)
+    forward(5, 0)
+    forward(4, 0)
     for d in (3, 5, 4):
         forward(d, 1)
 
@@ -391,7 +392,7 @@
 
     def fin_copy(chunk):
         span = pl.ds(chunk * HALF, HALF)
-        return remote(fin_out.at[span], fin_in.at[span], fin_send.at[chunk], fin_recv.at[chunk], at(dr=1))
+        return remote(fin_out.at[span], fin_other.at[span], fin_send.at[chunk], fin_recv.at[chunk], at(dr=1))
 
     @pl.when(lane == 0)
     def _():
@@ -411,12 +412,11 @@
             value = value + root_in[DIRECT[d], halves[chunk]].astype(F32)
         fin_out[halves[chunk]] = value.astype(BF16)
         go(fin_copy(chunk))
+    own_fin = pltpu.make_async_copy(fin_out, fin_own, local_sem.at[8])
+    own_fin.start()
 
     for chunk in range(2):
         fin_copy(chunk).wait_recv()
-    done[...] = (fin_out[...].astype(F32) + fin_in[...].astype(F32)).astype(BF16)
-    own_igrad = pltpu.make_async_copy(done, igrad, local_sem.at[8])
-    own_igrad.start()
 
     @pl.when(lane == 1)
     def _():
@@ -431,13 +431,13 @@
         g4_copy(dz).wait_recv()
     own_hid.wait()
     own_wgrad.wait()
-    own_igrad.wait()
-
-
-def hand_over(hid, wgrad, igrad, hid_to, wgrad_to, igrad_to):
+    own_fin.wait()
+
+
+def hand_over(hid, wgrad, fin_own, fin_other, hid_to, wgrad_to, igrad_to):
     hid_to[...] = hid[...]
     wgrad_to[...] = wgrad[...]
-    igrad_to[...] = igrad[...]
+    igrad_to[...] = (fin_own[...].astype(F32) + fin_other[...].astype(F32)).astype(BF16)
 
 
 def body(features_t, tile_values, tile_rows, tile_cols, tile_count, weight, cotangent_t):
@@ -452,9 +452,9 @@
     )
     results = pl.pallas_call(
         kernel,
-        out_shape=out_shape,
+        out_shape=(*out_shape, out_shape[2]),
         in_specs=[anywhere] * 7,
-        out_specs=(anywhere, anywhere, anywhere),
+        out_specs=(anywhere,) * 4,
         scratch_shapes=[
             pltpu.SMEM((SLOTS, 1, PARTS), jnp.int32),
             pltpu.SMEM((SLOTS, 1, PARTS), jnp.int32),
@@ -486,8 +486,6 @@
             vmem((2, 2, *panel), BF16),
             vmem((5, *panel), BF16),
             vmem((5, *panel), BF16),
-            vmem(panel, BF16),
-            vmem(panel, BF16),
             vmem(panel, BF16),
             dma((16,)), dma((9,)), dma((5, 2)), dma((5, 2)), dma((2, 3)), dma((2, 3)), dma((RING,)), dma((RING,)),
             dma((SIDE,)), dma((SIDE,)), dma((SIDE,)), dma((SIDE,)),
@@ -506,7 +504,7 @@
     return pl.pallas_call(
         hand_over,
         out_shape=out_shape,
-        in_specs=[pl.BlockSpec(memory_space=vmem)] * 3,
+        in_specs=[pl.BlockSpec(memory_space=vmem)] * 4,
         out_specs=(pl.BlockSpec(memory_space=vmem),) * 3,
     )(*results)
 

time: 50.3 us -> 49.8 us (0.990)
  no operation moved by 1% of the time
where the time goes in v5:
time: 49.8 us; the launch traced here: 49.7 us
  Pallas kernels  49.1 us (99%)
  between operations  0.64 us (1%)
    pallas_call x1, Pallas kernels, body(): pl.pallas_call(kernel, out_shape=(*out_shape, out_shape[2]), in_specs=[an...  47.4 us
    pallas_call x1, Pallas kernels, body(): pl.pallas_call(hand_over, out_shape=out_shape, in_specs=[pl.BlockSpec(mem...  1.61 us

profile of v5, /device:TPU:1, one launch (start us, length us, event | category | flops | bytes accessed | tf_op | source)
XLA Modules:
  0.0 49.7 jit_solution(7404660315615685657)
XLA Ops:
  0.6 47.4 %shard_map.94 = (bf16[64,512]{1,0:T(8,128)(2,1)}, f32[64,256]{1,0:T(8,128)}, bf16[64,512]{1,0:T(8,128)(2,1)}, bf16[64,512]{1,0:T(8,128)(2,1)}) custom-call(bf16[64,512]{1,0:T(8,128)(2,1)} %feat.1, bf16[1,32,12,128,128]{4,3,2,1,0:T(8,128)(2,1)} %tiles.1, s32[12,1,32]{2,1,0:T(1,128)} %bitcast.2, s32[12,1,32]{2,1,0:T(1,128)} %bitcast.3, s32[1,32]{1,0:T(1,128)} %count_hbm.1, ...), custom_call_target="tpu_custom_call" | custom-call | tf_op jit(solution)/shard_map/pallas_call | solution.py:453
  48.1 1.6 %shard_map.95 = (bf16[64,512]{1,0:T(8,128)(2,1)}, f32[64,256]{1,0:T(8,128)}, bf16[64,512]{1,0:T(8,128)(2,1)}) custom-call(bf16[64,512]{1,0:T(8,128)(2,1)} %get-tuple-element.7.hid, f32[64,256]{1,0:T(8,128)} %get-tuple-element.8.wgrad, bf16[64,512]{1,0:T(8,128)(2,1)} %get-tuple-element.9.fin_own, bf16[64,512]{1,0:T(8,128)(2,1)} %get-tuple-element.10.fin_other), custom_call_target="tpu_custom_call" | custom-call | tf_op jit(solution)/shard_map/pallas_call | solution.py:504

commit v6 on v5

--- a/solution.py
+++ b/solution.py
@@ -331,13 +331,15 @@
         near_out[way, 0] = keep[3 if way == 0 else 5].astype(BF16)
         go(near_copy(way, way))
         go(near_copy(way, 1 - way))
-    for d in (1, 7, 0, 2, 6):
+    for d in (2, 6, 1, 7, 0):
         give(d)
-
+    take(2)
+    take(6)
     for d in (1, 7):
         take(d)
         root_out[DIRECT[d]] = keep[d].astype(BF16)
         go(root_copy(d, 0))
+
     take(0)
 
     @pl.when(lane == 1)
@@ -345,8 +347,6 @@
         root_out[DIRECT[0]] = keep[0].astype(BF16)
         root_copy(0, 0).start()
 
-    take(2)
-    take(6)
 
     for dz in range(1, RING):
         g2_copy(dz).wait_recv()

time: 49.8 us -> 49.8 us (level)
  no operation moved by 1% of the time
where the time goes in v6:
time: 49.8 us; the launch traced here: 49.7 us
  Pallas kernels  49.1 us (99%)
  between operations  0.64 us (1%)
    pallas_call x1, Pallas kernels, body(): pl.pallas_call(kernel, out_shape=(*out_shape, out_shape[2]), in_specs=[an...  47.4 us
    pallas_call x1, Pallas kernels, body(): pl.pallas_call(hand_over, out_shape=out_shape, in_specs=[pl.BlockSpec(mem...  1.61 us

profile of v6, /device:TPU:1, one launch (start us, length us, event | category | flops | bytes accessed | tf_op | source)
XLA Modules:
  0.0 49.7 jit_solution(1498046180799512407)
XLA Ops:
  0.6 47.4 %shard_map.94 = (bf16[64,512]{1,0:T(8,128)(2,1)}, f32[64,256]{1,0:T(8,128)}, bf16[64,512]{1,0:T(8,128)(2,1)}, bf16[64,512]{1,0:T(8,128)(2,1)}) custom-call(bf16[64,512]{1,0:T(8,128)(2,1)} %feat.1, bf16[1,32,12,128,128]{4,3,2,1,0:T(8,128)(2,1)} %tiles.1, s32[12,1,32]{2,1,0:T(1,128)} %bitcast.2, s32[12,1,32]{2,1,0:T(1,128)} %bitcast.3, s32[1,32]{1,0:T(1,128)} %count_hbm.1, ...), custom_call_target="tpu_custom_call" | custom-call | tf_op jit(solution)/shard_map/pallas_call | solution.py:453
  48.1 1.6 %shard_map.95 = (bf16[64,512]{1,0:T(8,128)(2,1)}, f32[64,256]{1,0:T(8,128)}, bf16[64,512]{1,0:T(8,128)(2,1)}) custom-call(bf16[64,512]{1,0:T(8,128)(2,1)} %get-tuple-element.7.hid, f32[64,256]{1,0:T(8,128)} %get-tuple-element.8.wgrad, bf16[64,512]{1,0:T(8,128)(2,1)} %get-tuple-element.9.fin_own, bf16[64,512]{1,0:T(8,128)(2,1)} %get-tuple-element.10.fin_other), custom_call_target="tpu_custom_call" | custom-call | tf_op jit(solution)/shard_map/pallas_call | solution.py:504
